TPU v7x, 512 devices: a whole 4x4x16 slice. The times are simulated.
512 devices in a mesh: band: 64 (over x, y, z_lo), mem: 8 (over z_hi, core).
Axes of the slice: x: 4, y: 4, z: 16 (z_hi: 4, z_lo: 4; z = z_hi * 4 + z_lo), core: 2. Of those that a mesh axis runs over, the one named last changes fastest.
Arguments:
- perturbations: bfloat16 [80, 32, 131072], P('mem', None, 'band'), may hold values from -0.59765625 to 0.59765625
- mode_weights: bfloat16 [80, 16, 131072], P('mem', None, 'band'), may hold values from -6 to 6
- vertical_modes: bfloat16 [32, 16], replicated, may hold values from -1.5 to 1.5
- interp_weights: bfloat16 [16384, 128, 128], P(('band', 'mem')), may hold values from -1 to 2, as said below
- source_rows: int32 [16384, 128], P(('band', 'mem')), may hold values from 0 to 6143, as said below
- live_tiles: int32 [64], P('band'), may hold values from 64 to 256
- fine_cotangent: bfloat16 [32, 2097152], P(None, ('band', 'mem')), may hold values from -6 to 6
Outputs:
- fine_increment: bfloat16 [32, 2097152], P(None, ('band', 'mem'))
- mode_gradient: bfloat16 [80, 16, 131072], P('mem', None, 'band')
Inputs may be any that keep to these rules, and one draw needn't show every extreme that they name: `source_rows`: the rows of one tile are distinct. `interp_weights`: each fine point's weights sum to one, and each fine point has at most 16 nonzero weights.
All inputs are finite; a program needn't handle non-finite values.
Results may differ from a plain program's by a relative error of at most 0.0049.
Values may be sent and summed in bfloat16 or wider, within the bound.
No kernel may reach another device: no remote copies, remote signals or barrier semaphores. Data moves between devices by JAX's collectives and lax.ppermute only.
A program may use at most 64 MiB of HBM per device.

v0:
```python
import jax
import jax.numpy as jnp
from jax import lax
from jax.sharding import PartitionSpec as P


def with_halo(cells, sides, width):
    for axis, dim in sides:
        count = lax.axis_size(axis)
        ends = count - 1
        head = lax.slice_in_dim(cells, 0, width, axis=dim)
        tail = lax.slice_in_dim(cells, cells.shape[dim] - width, cells.shape[dim], axis=dim)
        cells = jnp.concatenate(
            [
                lax.ppermute(tail, axis, [(i, (i + 1) % count) for i in range(ends)]),
                cells,
                lax.ppermute(head, axis, [((i + 1) % count, i) for i in range(ends)]),
            ],
            axis=dim,
        )
    return cells


def from_behind(block, axis, distance):
    devices = range(lax.axis_size(axis))
    route = [(i - distance, i) for i in devices if i - distance in devices]
    return lax.ppermute(block, axis, route)


def shards(
    perturbations,
    mode_weights,
    vertical_modes,
    interp_weights,
    source_rows,
    live_tiles,
    fine_cotangent,
):
    members, levels, grid_points = perturbations.shape
    tiles, row_count, width = interp_weights.shape
    alpha = jnp.einsum(
        "lm,kmp->klp", vertical_modes, mode_weights, preferred_element_type=jnp.float32
    )
    partial_sum = jnp.sum(perturbations * alpha, axis=0)
    total = lax.psum(partial_sum, "mem")
    extended = with_halo(total.astype(jnp.bfloat16), (("band", 1),), grid_points)
    block = jnp.take(extended, source_rows, axis=1)
    slots = lax.axis_index("mem") * tiles + jnp.arange(tiles, dtype=jnp.int32)
    keep = (slots < live_tiles[0])[None, :, None]
    fine = jnp.einsum("ltc,tcf->ltf", block, interp_weights, preferred_element_type=jnp.float32)
    fine_increment = jnp.where(keep, fine, 0.0).astype(jnp.bfloat16).reshape(levels, tiles * width)
    cot = fine_cotangent.reshape(levels, tiles, width)
    cot = jnp.where(keep, cot, jnp.zeros((), jnp.bfloat16))
    back = jnp.einsum("ltf,tcf->ltc", cot, interp_weights, preferred_element_type=jnp.float32)
    local_adj = (
        jnp.zeros((levels, 3 * grid_points), jnp.float32)
        .at[:, source_rows.reshape(-1)]
        .add(back.reshape(levels, -1))
    )
    summed = lax.psum(local_adj, "mem")
    from_above = from_behind(summed[:, :grid_points], "band", -1)
    from_below = from_behind(summed[:, 2 * grid_points :], "band", 1)
    adjoint = summed[:, grid_points : 2 * grid_points] + from_above + from_below
    product = perturbations.astype(jnp.float32) * adjoint[None]
    mode_gradient = jnp.einsum(
        "lm,klp->kmp", vertical_modes.astype(jnp.float32), product, precision=lax.Precision.HIGHEST
    )
    return (fine_increment, mode_gradient.astype(jnp.bfloat16))


def solution(mesh):
    placed = (
        P("mem", None, "band"),
        P("mem", None, "band"),
        P(),
        P(("band", "mem"), None, None),
        P(("band", "mem"), None),
        P("band"),
        P(None, ("band", "mem")),
    )
    return jax.shard_map(
        shards,
        mesh=mesh,
        in_specs=placed,
        out_specs=(P(None, ("band", "mem")), P("mem", None, "band")),
        check_vma=False,
    )
```

profile of v0, /device:TPU:7, one launch (start us, length us, event | category | flops | bytes accessed | tf_op | source)
XLA Modules:
  0.0 192.1 jit_solution(14443212985040243362)
XLA Ops:
  7.2 0.0 copy-start
  7.2 0.0 all-reduce.3.cloned.1.call-start
  8.0 0.4 copy-done
  8.4 1.6 convolution_bitcast_fusion.1
  10.1 0.8 copy.45
  10.9 1.6 copy.34
  12.6 0.0 copy-done.3
  12.6 24.2 %scatter_custom_fusion = f32[32,6144]{0,1:T(8,128)} fusion(s32[4096]{0:T(1024)S(1)} %bitcast.52, f32[4096,32]{1,0:T(8,128)S(1)} %copy.34, f32[]{:T(128)} %constant.13.clone.1), kind=kCustom, calls=%fused_computation.8 | custom fusion | flops 131072 | bytes 786436 | tf_op jit(solution)/shard_map/scatter-add | solution.py:58
  36.8 3.2 %copy.35 = f32[32,6144]{1,0:T(8,128)} copy(f32[32,6144]{0,1:T(8,128)} %scatter_custom_fusion) | data formatting | bytes 1572864 | tf_op jit(solution)/shard_map/scatter-add | solution.py:58
  39.9 0.0 all-reduce.3.cloned.1.call-update
  40.0 1.6 fusion.5
  41.6 49.0 %all-reduce.4 = bf16[32,2048]{1,0:T(8,128)(2,1)S(1)} all-reduce(f32[32,2048]{1,0:T(8,128)S(1)} %fusion.5), channel_id=1, replica_groups=mesh['band'=64,'mem'=8] {'mem'}, use_global_device_ids=true, to_apply=%region_1.0 | all-reduce | flops 65536 | bytes 393216 | tf_op jit(solution)/shard_map/psum | solution.py:45
  90.6 1.9 collective-permute-start
  92.5 8.2 %collective-permute-start.1 = (bf16[32,2048]{1,0:T(8,128)(2,1)S(1)}, bf16[32,2048]{1,0:T(8,128)(2,1)S(1)}, u32[]{:S(2)}, u32[]{:S(2)}) collective-permute-start(bf16[32,2048]{1,0:T(8,128)(2,1)S(1)} %all-reduce.4), channel_id=1, source_target_pairs={{8,0},{16,8},{24,16},{32,24},{40,32},{48,40},{56,48},{64,56},{72,6... | collective-permute-start | bytes 393224 | tf_op jit(solution)/shard_map/ppermute | solution.py:17
  100.7 0.6 compare_and_fusion
  101.3 50.8 %all-reduce.3.cloned.1.call-done = f32[32,6144]{1,0:T(8,128)} async-done(((f32[32,6144]{1,0:T(8,128)}), f32[32,6144]{1,0:T(8,128)}) %all-reduce.3.cloned.1.call-update) | async-done | bytes 786448 | tf_op jit(solution)/shard_map/psum | solution.py:60
  152.1 1.8 fusion.21
  153.9 7.5 %collective-permute-start.2 = (f32[32,2048]{1,0:T(8,128)}, f32[32,2048]{1,0:T(8,128)S(1)}, u32[]{:S(2)}, u32[]{:S(2)}) collective-permute-start(f32[32,2048]{1,0:T(8,128)} %get-tuple-element.2), channel_id=1, source_target_pairs={{8,0},{16,8},{24,16},{32,24},{40,32},{48,40},{56,48},{64,56},{72,6... | collective-permute-start | bytes 786440 | tf_op jit(solution)/shard_map/ppermute | solution.py:27
  161.5 1.9 %collective-permute-start.3 = (f32[32,2048]{1,0:T(8,128)S(1)}, f32[32,2048]{1,0:T(8,128)}, u32[]{:S(2)}, u32[]{:S(2)}) collective-permute-start(f32[32,2048]{1,0:T(8,128)S(1)} %get-tuple-element.3), channel_id=1, source_target_pairs={{0,8},{8,16},{16,24},{24,32},{32,40},{40,48},{48,56},{56,64},{64,7... | collective-permute-start | bytes 786440 | tf_op jit(solution)/shard_map/ppermute | solution.py:27
  163.4 0.0 collective-permute-done
  163.4 0.0 collective-permute-done.1
  163.4 0.8 copy.29
  164.3 0.0 copy-start.4
  164.3 0.0 copy-start.8
  164.3 14.9 %gather_fusion = bf16[4096,32]{1,0:T(8,128)(2,1)} fusion(bf16[32,6144]{0,1:T(8,128)(2,1)S(1)} %copy.29, s32[4096]{0:T(1024)S(1)} %bitcast_clamp_fusion), kind=kCustom, calls=%fused_computation | custom fusion | bytes 540672 | tf_op jit(solution)/shard_map/jit(_take)/gather | solution.py:47
  179.2 1.7 copy.30
  180.9 0.4 fusion.8
  181.3 0.8 copy.46
  182.1 0.0 collective-permute-done.2
  182.1 0.0 collective-permute-done.3
  182.1 1.1 fusion.10
  183.2 2.1 %fusion.2 = bf16[10,16,2048]{2,1,0:T(8,128)(2,1)} fusion(bf16[10,32,2048]{2,1,0:T(8,128)(2,1)S(1)} %copy-done.2, f32[32,2048]{1,0:T(8,128)S(1)} %fusion.10, bf16[32,16]{0,1:T(8,128)(2,1)S(1)} %copy-done.6), kind=kOutput, calls=%fused_computation.7 | convolution fusion | flops 127467520 | bytes 2229248 | tf_op jit(solution)/shard_map/lm,klp->kmp/dot_general | solution.py:65
  (17 shorter events, 0.1 us)
Async XLA Ops:
  7.2 1.2 copy-start
  7.2 145.0 %all-reduce.3.cloned.1.call-start = ((), (), s32[]{:S(2)}) async-start(), calls=%async_computation | async-start | bytes 1572864 | tf_op jit(solution)/shard_map/psum | solution.py:60
  8.4 2.5 %copy-start.7 = (pred[32]{0:T(512)(128)(4,1)}, pred[32]{0:T(512)(128)(4,1)S(1)}, u32[]{:S(2)}) copy-start(pred[32]{0:T(512)(128)(4,1)S(1)} %add_compare_fusion) | copy-start | bytes 100
  8.4 4.1 %copy-start.3 = (s32[32,128]{1,0:T(8,128)S(1)}, s32[32,128]{1,0:T(8,128)}, u32[]{:S(2)}) copy-start(s32[32,128]{1,0:T(8,128)} %param.11) | copy-start | bytes 49156
  36.7 3.2 %copy-start.1 = (bf16[10,32,2048]{2,1,0:T(8,128)(2,1)S(1)}, bf16[10,32,2048]{2,1,0:T(8,128)(2,1)}, u32[]{:S(2)}) copy-start(bf16[10,32,2048]{2,1,0:T(8,128)(2,1)} %param.7) | copy-start | bytes 3932164
  36.8 3.2 %copy-start.5 = (bf16[32,16]{0,1:T(8,128)(2,1)S(1)}, bf16[32,16]{0,1:T(8,128)(2,1)}, u32[]{:S(2)}) copy-start(bf16[32,16]{0,1:T(8,128)(2,1)} %param.9) | copy-start | bytes 3076
  90.6 72.8 %collective-permute-start = (bf16[32,2048]{1,0:T(8,128)(2,1)S(1)}, bf16[32,2048]{1,0:T(8,128)(2,1)S(1)}, u32[]{:S(2)}, u32[]{:S(2)}) collective-permute-start(bf16[32,2048]{1,0:T(8,128)(2,1)S(1)} %all-reduce.4), channel_id=1, source_target_pairs={{0,8},{8,16},{16,24},{24,32},{32,40},{40,48},{48,56},{56,64},{64,7... | collective-permute-start | bytes 393224 | tf_op jit(solution)/shard_map/ppermute | solution.py:15
  92.5 70.9 %collective-permute-start.1 = (bf16[32,2048]{1,0:T(8,128)(2,1)S(1)}, bf16[32,2048]{1,0:T(8,128)(2,1)S(1)}, u32[]{:S(2)}, u32[]{:S(2)}) collective-permute-start(bf16[32,2048]{1,0:T(8,128)(2,1)S(1)} %all-reduce.4), channel_id=1, source_target_pairs={{8,0},{16,8},{24,16},{32,24},{40,32},{48,40},{56,48},{64,56},{72,6... | collective-permute-start | bytes 393224 | tf_op jit(solution)/shard_map/ppermute | solution.py:17
  153.9 28.1 %collective-permute-start.2 = (f32[32,2048]{1,0:T(8,128)}, f32[32,2048]{1,0:T(8,128)S(1)}, u32[]{:S(2)}, u32[]{:S(2)}) collective-permute-start(f32[32,2048]{1,0:T(8,128)} %get-tuple-element.2), channel_id=1, source_target_pairs={{8,0},{16,8},{24,16},{32,24},{40,32},{48,40},{56,48},{64,56},{72,6... | collective-permute-start | bytes 786440 | tf_op jit(solution)/shard_map/ppermute | solution.py:27
  161.5 20.6 %collective-permute-start.3 = (f32[32,2048]{1,0:T(8,128)S(1)}, f32[32,2048]{1,0:T(8,128)}, u32[]{:S(2)}, u32[]{:S(2)}) collective-permute-start(f32[32,2048]{1,0:T(8,128)S(1)} %get-tuple-element.3), channel_id=1, source_target_pairs={{0,8},{8,16},{16,24},{24,32},{32,40},{40,48},{48,56},{56,64},{64,7... | collective-permute-start | bytes 786440 | tf_op jit(solution)/shard_map/ppermute | solution.py:27
  164.3 16.6 %copy-start.4 = (pred[32,128]{1,0:T(8,128)(4,1)S(1)}, pred[32,128]{1,0:T(8,128)(4,1)}, u32[]{:S(2)}) copy-start(pred[32,128]{1,0:T(8,128)(4,1)} %compare_and_fusion) | copy-start | bytes 12292
  164.3 16.6 %copy-start.8 = (pred[32]{0:T(512)(128)(4,1)S(1)}, pred[32]{0:T(512)(128)(4,1)}, u32[]{:S(2)}) copy-start(pred[32]{0:T(512)(128)(4,1)} %copy-done.7) | copy-start | bytes 100
  179.2 3.9 %copy-start.2 = (bf16[10,32,2048]{2,1,0:T(8,128)(2,1)S(1)}, bf16[10,32,2048]{2,1,0:T(8,128)(2,1)}, u32[]{:S(2)}) copy-start(bf16[10,32,2048]{2,1,0:T(8,128)(2,1)} %param.7) | copy-start | bytes 3932164
  179.2 3.9 %copy-start.6 = (bf16[32,16]{0,1:T(8,128)(2,1)S(1)}, bf16[32,16]{0,1:T(8,128)(2,1)}, u32[]{:S(2)}) copy-start(bf16[32,16]{0,1:T(8,128)(2,1)} %param.9) | copy-start | bytes 3076
Sparse Core Ops, SparseCore 0:
  40.1 112.0 all-reduce.2
where the time goes:
time: 192 us
  waiting for transfers between devices  50.9 us (27%)
  blocking collectives  49 us (26%)
  local copies, waits for them, and re-layouts  26.1 us (14%)
  other arithmetic  25.9 us (13%)
  starting transfers between devices  19.6 us (10%)
  between operations  14.9 us (8%)
  matrix products  5.76 us (3%)
    psum x1, waiting for transfers between devices, shards(): summed = lax.psum(local_adj, 'mem')  50.8 us
    psum x1, blocking collectives, shards(): total = lax.psum(partial_sum, 'mem')  49 us
    scatter-add x1, other arithmetic, shards(): local_adj = jnp.zeros((levels, 3 * grid_points), jnp.float32).at[:, sourc...  24.2 us
    gather x2, local copies, waits for them, and re-layouts, shards(): block = jnp.take(extended, source_rows, axis=1)  16.6 us
    ppermute x2, starting transfers between devices, from_behind(): return lax.ppermute(block, axis, route)  9.46 us
    ppermute x1, starting transfers between devices, with_halo(): lax.ppermute(head, axis, [((i + 1) % count, i) for i in range(ends)])  8.17 us
  transfers between devices with their start and end apart: 5, of which 1 were waited for; matrix products, arithmetic and copies ran while one was open for 12% of the time, Pallas kernels for 0%

commit v1 on v0

v1 whole, which is shorter than its diff:
```python
import functools

import jax
import jax.numpy as jnp
from jax import lax
from jax.experimental import pallas as pl
from jax.experimental.pallas import tpu as pltpu
from jax.sharding import PartitionSpec as P

F32 = jnp.float32
BF16 = jnp.bfloat16
LANES = 256
BAND = 2048
CHUNKS = BAND // LANES
GROUP = 8


def scatter_kernel(live_ref, rows_ref, weights_ref, cot_ref, out_ref):
    tiles, width, _ = weights_ref.shape
    levels = cot_ref.shape[0]
    chunks = out_ref.shape[0] // levels
    first = lax.axis_index("mem") * tiles
    live = live_ref[0]
    lane = lax.broadcasted_iota(jnp.int32, (width, LANES), 1)
    turned = rows_ref[...].T
    for start in range(0, tiles, GROUP):
        spread, hot = [], []
        for tile in range(start, start + GROUP):
            cot = cot_ref[:, tile * width : (tile + 1) * width]
            back = lax.dot_general(
                cot, weights_ref[tile], (((1,), (1,)), ((), ())), preferred_element_type=F32
            )
            back = jnp.where(first + tile < live, back, 0.0)
            chunk = rows_ref[tile : tile + 1, :] // LANES
            spread.append(
                jnp.concatenate(
                    [jnp.where(chunk == k, back, 0.0).astype(BF16) for k in range(chunks)], axis=0
                )
            )
            column = turned[:, tile : tile + 1] % LANES
            hot.append(jnp.where(column == lane, 1.0, 0.0).astype(BF16))
        part = jnp.dot(
            jnp.concatenate(spread, axis=1),
            jnp.concatenate(hot, axis=0),
            preferred_element_type=F32,
        )
        if start == 0:
            total = part
        else:
            total = total + part
    out_ref[...] = total.astype(BF16)


def scatter(live_tiles, source_rows, interp_weights, fine_cotangent):
    levels = fine_cotangent.shape[0]
    vmem = pl.BlockSpec(memory_space=pltpu.VMEM)
    return pl.pallas_call(
        scatter_kernel,
        out_shape=jax.ShapeDtypeStruct((3 * CHUNKS * levels, LANES), BF16),
        in_specs=[pl.BlockSpec(memory_space=pltpu.SMEM), vmem, vmem, vmem],
        out_specs=vmem,
        compiler_params=pltpu.CompilerParams(vmem_limit_bytes=40 * 2**20),
        cost_estimate=pl.CostEstimate(flops=2 * 10**9, bytes_accessed=2 * 10**6, transcendentals=0),
        name="scatter",
    )(live_tiles, source_rows, interp_weights, fine_cotangent)


def partial_kernel(pert_ref, weights_ref, modes_ref, out_ref):
    members, levels, points = pert_ref.shape
    for chunk in range(points // LANES):
        at = slice(chunk * LANES, (chunk + 1) * LANES)
        total = jnp.zeros((levels, LANES), F32)
        for k in range(members):
            alpha = jnp.dot(modes_ref[...], weights_ref[k, :, at], preferred_element_type=F32)
            total = total + pert_ref[k, :, at].astype(F32) * alpha
        out_ref[chunk * levels : (chunk + 1) * levels, :] = total.astype(BF16)


def partial_sum(perturbations, mode_weights, vertical_modes):
    members, levels, points = perturbations.shape
    vmem = pl.BlockSpec(memory_space=pltpu.VMEM)
    return pl.pallas_call(
        partial_kernel,
        out_shape=jax.ShapeDtypeStruct((points // LANES * levels, LANES), BF16),
        in_specs=[vmem, vmem, vmem],
        out_specs=vmem,
        compiler_params=pltpu.CompilerParams(vmem_limit_bytes=40 * 2**20),
        cost_estimate=pl.CostEstimate(flops=2 * 10**9, bytes_accessed=3 * 10**6, transcendentals=0),
        name="partial_sum",
    )(perturbations, mode_weights, vertical_modes)


def fine_kernel(live_ref, rows_ref, weights_ref, middle_ref, sides_ref, out_ref):
    tiles, width, _ = weights_ref.shape
    levels = out_ref.shape[0]
    first = lax.axis_index("mem") * tiles
    live = live_ref[0]
    line = lax.broadcasted_iota(jnp.int32, (LANES, 2 * width), 0)
    extended = jnp.concatenate([sides_ref[0], middle_ref[...], sides_ref[1]], axis=0)
    for tile in range(0, tiles, 2):
        rows = jnp.concatenate([rows_ref[tile : tile + 1, :], rows_ref[tile + 1 : tile + 2, :]], axis=1)
        chunk, column = rows // LANES, rows % LANES
        hot = jnp.where(column == line, 1.0, 0.0).astype(BF16)
        picked = jnp.dot(extended, hot, preferred_element_type=F32)
        block = jnp.zeros((levels, 2 * width), F32)
        for k in range(extended.shape[0] // levels):
            block = jnp.where(chunk == k, picked[k * levels : (k + 1) * levels], block)
        block = block.astype(BF16)
        for i in range(2):
            fine = jnp.dot(
                block[:, i * width : (i + 1) * width], weights_ref[tile + i], preferred_element_type=F32
            )
            fine = jnp.where(first + tile + i < live, fine, 0.0)
            out_ref[:, (tile + i) * width : (tile + i + 1) * width] = fine.astype(BF16)


def fine_sum(live_tiles, source_rows, interp_weights, middle, sides):
    tiles, width, _ = interp_weights.shape
    levels = middle.shape[0] // CHUNKS
    vmem = pl.BlockSpec(memory_space=pltpu.VMEM)
    return pl.pallas_call(
        fine_kernel,
        out_shape=jax.ShapeDtypeStruct((levels, tiles * width), BF16),
        in_specs=[pl.BlockSpec(memory_space=pltpu.SMEM), vmem, vmem, vmem, vmem],
        out_specs=vmem,
        compiler_params=pltpu.CompilerParams(vmem_limit_bytes=40 * 2**20),
        cost_estimate=pl.CostEstimate(flops=2 * 10**9, bytes_accessed=2 * 10**6, transcendentals=0),
        name="fine_sum",
    )(live_tiles, source_rows, interp_weights, middle, sides)


def gradient_kernel(pert_ref, modes_ref, adjoint_ref, out_ref):
    members, levels, points = pert_ref.shape
    modes = jnp.concatenate([modes_ref[...], modes_ref[...]], axis=0)
    for chunk in range(points // LANES):
        at = slice(chunk * LANES, (chunk + 1) * LANES)
        adjoint = adjoint_ref[chunk * levels : (chunk + 1) * levels, :].astype(F32)
        for k in range(members):
            product = pert_ref[k, :, at].astype(F32) * adjoint
            high = product.astype(BF16)
            low = (product - high.astype(F32)).astype(BF16)
            both = jnp.concatenate([high, low], axis=0)
            out_ref[k, :, at] = lax.dot_general(
                modes, both, (((0,), (0,)), ((), ())), preferred_element_type=F32
            ).astype(BF16)


def gradient(perturbations, vertical_modes, adjoint):
    members, levels, points = perturbations.shape
    vmem = pl.BlockSpec(memory_space=pltpu.VMEM)
    return pl.pallas_call(
        gradient_kernel,
        out_shape=jax.ShapeDtypeStruct((members, vertical_modes.shape[1], points), BF16),
        in_specs=[vmem, vmem, vmem],
        out_specs=vmem,
        compiler_params=pltpu.CompilerParams(vmem_limit_bytes=40 * 2**20),
        cost_estimate=pl.CostEstimate(flops=2 * 10**9, bytes_accessed=3 * 10**6, transcendentals=0),
        name="gradient",
    )(perturbations, vertical_modes, adjoint)


def shards(
    perturbations,
    mode_weights,
    vertical_modes,
    interp_weights,
    source_rows,
    live_tiles,
    fine_cotangent,
):
    bands, mems = lax.axis_size("band"), lax.axis_size("mem")
    core = lax.axis_index("mem") % 2
    pairs = [[m, m + 1] for m in range(0, mems, 2)]
    chips = [list(range(c, mems, 2)) for c in range(2)]
    route = [
        (b * mems + m, (b + 1 - 2 * (m % 2)) * mems + m)
        for b in range(bands)
        for m in range(mems)
        if 0 <= b + 1 - 2 * (m % 2) < bands
    ]
    to_pair = functools.partial(lax.all_gather, axis_name="mem", axis_index_groups=pairs)
    to_chips = functools.partial(lax.all_gather, axis_name="mem", axis_index_groups=chips)
    to_bands = functools.partial(lax.ppermute, axis_name=("band", "mem"), perm=route)

    local = scatter(live_tiles, source_rows, interp_weights, fine_cotangent)
    both = to_pair(local)
    rows = local.shape[0] // 3
    here = both[0].astype(F32) + both[1].astype(F32)
    send = lax.dynamic_slice_in_dim(here, (1 - core) * 2 * rows, rows, 0).astype(BF16)
    centre = here[rows : 2 * rows]
    came = to_bands(send)
    part = partial_sum(perturbations, mode_weights, vertical_modes)
    both = to_pair(jnp.stack([part, came])).astype(F32)
    half = rows // 2
    both = lax.dynamic_slice_in_dim(both, core * half, half, 2)
    centre = lax.dynamic_slice_in_dim(centre, core * half, half, 0)
    sums = jnp.stack([both[0, 0] + both[1, 0], both[0, 1] + both[1, 1] + centre]).astype(BF16)
    sums = jnp.sum(to_chips(sums).astype(F32), axis=0).astype(BF16)
    both = to_pair(sums)
    middle = both[:, 0].reshape(rows, LANES)
    adjoint = both[:, 1].reshape(rows, LANES)
    came = to_bands(middle)
    mode_gradient = gradient(perturbations, vertical_modes, adjoint)
    sides = to_pair(came)
    fine_increment = fine_sum(live_tiles, source_rows, interp_weights, middle, sides)
    return (fine_increment, mode_gradient)


def solution(mesh):
    placed = (
        P("mem", None, "band"),
        P("mem", None, "band"),
        P(),
        P(("band", "mem"), None, None),
        P(("band", "mem"), None),
        P("band"),
        P(None, ("band", "mem")),
    )
    return jax.shard_map(
        shards,
        mesh=mesh,
        in_specs=placed,
        out_specs=(P(None, ("band", "mem")), P("mem", None, "band")),
        check_vma=False,
    )
```

time: 192 us -> 81.5 us (0.42)
  waiting for transfers between devices: 50.9 us -> 1.74 us
  other arithmetic: 25.9 us -> 1.33 us
  local copies, waits for them, and re-layouts: 26.1 us -> 3.99 us
  between operations: 14.9 us -> 1.46 us
  Pallas kernels: 0 us -> 11.1 us
  matrix products: 5.76 us -> 0 us
  blocking collectives: 49 us -> 43.8 us
    psum x1 -> x0, waiting for transfers between devices: 50.8 us -> none  [shards(): summed = lax.psum(local_adj, 'mem')]
    psum x1 -> x0, blocking collectives: 49 us -> none  [shards(): total = lax.psum(partial_sum, 'mem')]
    all_gather x0 -> x5, blocking collectives: none -> 43.8 us  [the longest x1 30.4 us: shards(): sums = jnp.sum(to_chips(sums).astype(F32), axis=0).astype(BF16)]
    scatter-add x1 -> x0, other arithmetic: 24.2 us -> none  [shards(): local_adj = jnp.zeros((levels, 3 * grid_points), jnp.float32).at[:, sourc...]
    gather x2 -> x0, local copies, waits for them, and re-layouts: 16.6 us -> none  [shards(): block = jnp.take(extended, source_rows, axis=1)]
    pallas_call x0 -> x4, Pallas kernels: none -> 11.1 us  [the longest x1 5.57 us: fine_sum(): pl.pallas_call(fine_kernel, out_shape=jax.ShapeDtypeStruct((levels, tiles...]
    dot_general x4 -> x0, matrix products: 5.76 us -> none  [the longest x1 2.09 us: shards(): jnp.einsum('lm,klp->kmp', vertical_modes.astype(jnp.float32), product, pr...]
    reshape x3 -> x0, local copies, waits for them, and re-layouts: 3.24 us -> none  [the longest x2 2.48 us: shards(): back.reshape(levels, -1)]
  transfers between devices with their start and end apart: 5 -> 2, of which waited for: 1 -> 2; matrix products, arithmetic and copies ran while one was open for 12% -> 0% of each run, Pallas kernels for 0% -> 2%
where the time goes in v1:
time: 81.5 us; the launch traced here: 81.2 us
  blocking collectives  43.8 us (54%)
  starting transfers between devices  17.8 us (22%)
  Pallas kernels  11.1 us (14%)
  local copies, waits for them, and re-layouts  3.99 us (5%)
  waiting for transfers between devices  1.74 us (2%)
  between operations  1.46 us (2%)
  other arithmetic  1.33 us (2%)
    all_gather x1, blocking collectives, shards(): sums = jnp.sum(to_chips(sums).astype(F32), axis=0).astype(BF16)  30.4 us
    ppermute x1, starting transfers between devices, shards(): came = to_bands(send)  8.96 us
    ppermute x1, starting transfers between devices, shards(): came = to_bands(middle)  8.8 us
    pallas_call x1, Pallas kernels, fine_sum(): pl.pallas_call(fine_kernel, out_shape=jax.ShapeDtypeStruct((levels, tiles...  5.57 us
    all_gather x1, blocking collectives, shards(): both = to_pair(jnp.stack([part, came])).astype(F32)  4.32 us
    all_gather x1, blocking collectives, shards(): sides = to_pair(came)  4.13 us
    pallas_call x1, Pallas kernels, scatter(): pl.pallas_call(scatter_kernel, out_shape=jax.ShapeDtypeStruct((3 * CHUNKS...  3.61 us
    unnamed x19, local copies, waits for them, and re-layouts  3.3 us
  transfers between devices with their start and end apart: 2, of which 2 were waited for; matrix products, arithmetic and copies ran while one was open for 0% of the time, Pallas kernels for 2%

profile of v1, /device:TPU:7, one launch (start us, length us, event | category | flops | bytes accessed | tf_op | source)
XLA Modules:
  0.0 81.2 jit_solution(10644579479389814934)
XLA Ops:
  1.3 0.0 copy-start.1
  1.3 1.2 %copy-done.1 = bf16[32,128,128]{2,1,0:T(8,128)(2,1)S(1)} copy-done((bf16[32,128,128]{2,1,0:T(8,128)(2,1)S(1)}, bf16[32,128,128]{2,1,0:T(8,128)(2,1)}, u32[]{:S(2)}) %copy-start.1) | copy-done | bytes 1048600
  2.5 0.9 %copy-done.4 = bf16[32,4096]{1,0:T(8,128)(2,1)S(1)} copy-done((bf16[32,4096]{1,0:T(8,128)(2,1)S(1)}, bf16[32,4096]{1,0:T(8,128)(2,1)}, u32[]{:S(2)}) %copy-start.4) | copy-done | bytes 262168
  3.5 0.7 copy-done.5
  4.2 3.6 %scatter.1 = bf16[768,256]{1,0:T(8,128)(2,1)S(1)} custom-call(s32[1]{0:T(128)S(6)} %copy.15.live_ref, s32[32,128]{1,0:T(8,128)S(1)} %copy-done.5, bf16[32,128,128]{2,1,0:T(8,128)(2,1)S(1)} %copy-done.1, bf16[32,4096]{1,0:T(8,128)(2,1)S(1)} %copy-done.4), custom_call_target="tpu_custom_call" | custom-call | flops 2000000000 | bytes 2000000 | tf_op jit(solution)/shard_map/scatter/pallas_call | solution.py:57
  7.8 2.7 %all-gather = bf16[1536,256]{1,0:T(8,128)(2,1)S(1)} all-gather(bf16[768,256]{1,0:T(8,128)(2,1)S(1)} %scatter.1), channel_id=2, replica_groups={{0,1},{2,3},{4,5},{6,7},{8,9},{10,11},{12,13},{14,15},{16,17},{18,19},{..., dimensions={0}, use_global_device_ids=true | all-gather | bytes 1179648 | tf_op jit(solution)/shard_map/all_gather | solution.py:186
  10.5 0.1 convert_add_fusion
  10.6 0.0 copy-start.8
  10.6 0.0 copy-start
  10.6 0.0 copy-start.3
  10.6 0.7 dynamic-slice_convert_fusion.1
  11.3 9.0 %collective-permute-start = (bf16[256,256]{1,0:T(8,128)(2,1)}, bf16[256,256]{1,0:T(8,128)(2,1)}, u32[]{:S(2)}, u32[]{:S(2)}) collective-permute-start(bf16[256,256]{1,0:T(8,128)(2,1)} %dynamic-slice_convert_fusion.1), channel_id=1, source_target_pairs={{0,8},{2,10},{4,12},{6,14},{8,16},{9,1},{10,18},{11,3},{12,20},{13... | collective-permute-start | bytes 393224 | tf_op jit(solution)/shard_map/ppermute | solution.py:191
  20.3 0.1 fusion.5
  20.3 0.0 copy-start.7
  20.4 0.0 copy-done.8
  20.4 0.1 copy.13.modes_ref
  20.5 0.0 copy-done
  20.5 0.5 partial_sum.1
  20.9 0.3 copy-done.7
  21.2 1.3 %collective-permute-done = bf16[256,256]{1,0:T(8,128)(2,1)} collective-permute-done((bf16[256,256]{1,0:T(8,128)(2,1)}, bf16[256,256]{1,0:T(8,128)(2,1)}, u32[]{:S(2)}, u32[]{:S(2)}) %collective-permute-start) | collective-permute-done | bytes 131104 | tf_op jit(solution)/shard_map/ppermute | solution.py:191
  22.5 1.0 %pad_maximum_fusion = bf16[2,256,256]{2,1,0:T(8,128)(2,1)S(1)} fusion(bf16[1,256,256]{2,1,0:T(8,128)(2,1)} %bitcast.1, bf16[1,256,256]{2,1,0:T(8,128)(2,1)S(1)} %bitcast.28), kind=kLoop, calls=%fused_computation.2 | loop fusion | flops 131072 | bytes 524288 | tf_op jit(solution)/shard_map/stack | solution.py:193
  23.5 4.3 %all-gather.1 = bf16[4,256,256]{2,1,0:T(8,128)(2,1)S(1)} all-gather(bf16[2,256,256]{2,1,0:T(8,128)(2,1)S(1)} %pad_maximum_fusion), channel_id=3, replica_groups={{0,1},{2,3},{4,5},{6,7},{8,9},{10,11},{12,13},{14,15},{16,17},{18,19},{..., dimensions={0}, use_global_device_ids=true | all-gather | bytes 786432 | tf_op jit(solution)/shard_map/all_gather | solution.py:193
  27.9 30.4 %all_gather.32 = bf16[4,2,128,256]{3,2,1,0:T(8,128)(2,1)S(1)} all-gather(bf16[1,2,128,256]{3,2,1,0:T(8,128)(2,1)S(1)} %pad_maximum_fusion.1), channel_id=1, replica_groups={{0,2,4,6},{1,3,5,7},{8,10,12,14},{9,11,13,15},{16,18,20,22},{17,19,21,2..., dimensions={0}, use_global_device_ids=true | all-gather | bytes 655360 | tf_op jit(solution)/shard_map/all_gather | solution.py:198
  58.3 0.1 reduce_sum.12
  58.4 2.3 %all-gather.2 = bf16[4,128,256]{2,1,0:T(8,128)(2,1)S(1)} all-gather(bf16[2,128,256]{2,1,0:T(8,128)(2,1)S(1)} %reduce_sum.12), channel_id=4, replica_groups={{0,1},{2,3},{4,5},{6,7},{8,9},{10,11},{12,13},{14,15},{16,17},{18,19},{..., dimensions={0}, use_global_device_ids=true | all-gather | bytes 393216 | tf_op jit(solution)/shard_map/all_gather | solution.py:199
  60.7 8.8 %collective-permute-start.1 = (bf16[256,256]{1,0:T(8,128)(2,1)S(1)}, bf16[256,256]{1,0:T(8,128)(2,1)S(1)}, u32[]{:S(2)}, u32[]{:S(2)}) collective-permute-start(bf16[256,256]{1,0:T(8,128)(2,1)S(1)} %bitcast.25), channel_id=1, source_target_pairs={{0,8},{2,10},{4,12},{6,14},{8,16},{9,1},{10,18},{11,3},{12,20},{13... | collective-permute-start | bytes 393224 | tf_op jit(solution)/shard_map/ppermute | solution.py:202
  69.5 0.0 copy-start.2
  69.5 0.0 copy-start.6
  69.5 1.4 %gradient.1 = bf16[10,16,2048]{2,1,0:T(8,128)(2,1)} custom-call(bf16[10,32,2048]{2,1,0:T(8,128)(2,1)S(1)} %copy-done, bf16[32,16]{1,0:T(8,128)(2,1)S(1)} %copy.13.modes_ref, bf16[256,256]{1,0:T(8,128)(2,1)S(1)} %bitcast.27), custom_call_target="tpu_custom_call" | custom-call | flops 2000000000 | bytes 3000000 | tf_op jit(solution)/shard_map/gradient/pallas_call | solution.py:151
  71.0 0.5 collective-permute-done.1
  71.4 4.1 %all-gather.3 = bf16[512,256]{1,0:T(8,128)(2,1)S(1)} all-gather(bf16[256,256]{1,0:T(8,128)(2,1)S(1)} %collective-permute-done.1), channel_id=5, replica_groups={{0,1},{2,3},{4,5},{6,7},{8,9},{10,11},{12,13},{14,15},{16,17},{18,19},{..., dimensions={0}, use_global_device_ids=true | all-gather | bytes 393216 | tf_op jit(solution)/shard_map/all_gather | solution.py:204
  75.6 5.6 %fine_sum.1 = bf16[32,4096]{1,0:T(8,128)(2,1)} custom-call(s32[1]{0:T(128)S(6)} %copy.15.live_ref, s32[32,128]{1,0:T(8,128)S(1)} %copy-done.6, bf16[32,128,128]{2,1,0:T(8,128)(2,1)S(1)} %copy-done.2, bf16[256,256]{1,0:T(8,128)(2,1)S(1)} %bitcast.26, bf16[2,256,256]{2,1,0:T(8,128)(2,1)S(1)} %bitcast.24), custom_call_target="tpu_custom_call" | custom-call | flops 2000000000 | bytes 2000000 | tf_op jit(solution)/shard_map/fine_sum/pallas_call | solution.py:121
  (12 shorter events, 0.1 us)
Async XLA Ops:
  1.3 1.2 %copy-start.1 = (bf16[32,128,128]{2,1,0:T(8,128)(2,1)S(1)}, bf16[32,128,128]{2,1,0:T(8,128)(2,1)}, u32[]{:S(2)}) copy-start(bf16[32,128,128]{2,1,0:T(8,128)(2,1)} %weights_ref.5) | copy-start | bytes 3145732
  2.5 0.9 %copy-start.4 = (bf16[32,4096]{1,0:T(8,128)(2,1)S(1)}, bf16[32,4096]{1,0:T(8,128)(2,1)}, u32[]{:S(2)}) copy-start(bf16[32,4096]{1,0:T(8,128)(2,1)} %cot_ref.1) | copy-start | bytes 786436
  3.5 0.7 copy-start.5
  10.6 9.8 %copy-start.8 = (bf16[32,16]{0,1:T(8,128)(2,1)S(1)}, bf16[32,16]{0,1:T(8,128)(2,1)}, u32[]{:S(2)}) copy-start(bf16[32,16]{0,1:T(8,128)(2,1)} %param.9) | copy-start | bytes 3076
  10.6 9.9 %copy-start = (bf16[10,32,2048]{2,1,0:T(8,128)(2,1)S(1)}, bf16[10,32,2048]{2,1,0:T(8,128)(2,1)}, u32[]{:S(2)}) copy-start(bf16[10,32,2048]{2,1,0:T(8,128)(2,1)} %pert_ref.3) | copy-start | bytes 3932164
  10.6 9.9 %copy-start.3 = (bf16[10,16,2048]{2,1,0:T(8,128)(2,1)S(1)}, bf16[10,16,2048]{2,1,0:T(8,128)(2,1)}, u32[]{:S(2)}) copy-start(bf16[10,16,2048]{2,1,0:T(8,128)(2,1)} %weights_ref.3) | copy-start | bytes 1966084
  11.3 11.2 %collective-permute-start = (bf16[256,256]{1,0:T(8,128)(2,1)}, bf16[256,256]{1,0:T(8,128)(2,1)}, u32[]{:S(2)}, u32[]{:S(2)}) collective-permute-start(bf16[256,256]{1,0:T(8,128)(2,1)} %dynamic-slice_convert_fusion.1), channel_id=1, source_target_pairs={{0,8},{2,10},{4,12},{6,14},{8,16},{9,1},{10,18},{11,3},{12,20},{13... | collective-permute-start | bytes 393224 | tf_op jit(solution)/shard_map/ppermute | solution.py:191
  20.3 0.9 %copy-start.7 = (f32[1,768,256]{2,1,0:T(8,128)}, f32[1,768,256]{2,1,0:T(8,128)S(1)}, u32[]{:S(2)}) copy-start(f32[1,768,256]{2,1,0:T(8,128)S(1)} %fusion.5) | copy-start | bytes 2359300
  22.5 5.4 %slice-start = ((f32[1,768,256]{2,1,0:T(8,128)}), f32[1,256,256]{2,1,0:T(8,128)S(1)}, s32[]{:S(2)}) async-start(f32[1,768,256]{2,1,0:T(8,128)} %copy-done.7), calls=%async_computation | async-start | bytes 524288 | tf_op jit(solution)/shard_map/slice | solution.py:190
  60.7 10.7 %collective-permute-start.1 = (bf16[256,256]{1,0:T(8,128)(2,1)S(1)}, bf16[256,256]{1,0:T(8,128)(2,1)S(1)}, u32[]{:S(2)}, u32[]{:S(2)}) collective-permute-start(bf16[256,256]{1,0:T(8,128)(2,1)S(1)} %bitcast.25), channel_id=1, source_target_pairs={{0,8},{2,10},{4,12},{6,14},{8,16},{9,1},{10,18},{11,3},{12,20},{13... | collective-permute-start | bytes 393224 | tf_op jit(solution)/shard_map/ppermute | solution.py:202
  69.5 6.1 %copy-start.2 = (bf16[32,128,128]{2,1,0:T(8,128)(2,1)S(1)}, bf16[32,128,128]{2,1,0:T(8,128)(2,1)}, u32[]{:S(2)}) copy-start(bf16[32,128,128]{2,1,0:T(8,128)(2,1)} %weights_ref.5) | copy-start | bytes 3145732
  69.5 6.0 %copy-start.6 = (s32[32,128]{1,0:T(8,128)S(1)}, s32[32,128]{1,0:T(8,128)}, u32[]{:S(2)}) copy-start(s32[32,128]{1,0:T(8,128)} %rows_ref.3) | copy-start | bytes 49156

commit v2 on v0

v2 whole, which is shorter than its diff:
```python
import functools

import jax
import jax.numpy as jnp
from jax import lax
from jax.experimental import pallas as pl
from jax.experimental.pallas import tpu as pltpu
from jax.sharding import PartitionSpec as P

F32 = jnp.float32
BF16 = jnp.bfloat16
LANES = 256
BAND = 2048
CHUNKS = BAND // LANES
GROUP = 8
STEP = 4
NEAR = 4

CENTRE = range(CHUNKS, 2 * CHUNKS)
SIDES = [*range(CHUNKS), *range(2 * CHUNKS, 3 * CHUNKS)]


def compiled(kernel, out, in_specs, name, scratch=(), flops=2 * 10**9, mib=32):
    vmem = pl.BlockSpec(memory_space=pltpu.VMEM)
    return pl.pallas_call(
        kernel,
        out_shape=out,
        in_specs=in_specs,
        out_specs=jax.tree.map(lambda _: vmem, out),
        scratch_shapes=list(scratch),
        compiler_params=pltpu.CompilerParams(vmem_limit_bytes=int(mib * 2**20)),
        cost_estimate=pl.CostEstimate(flops=flops, bytes_accessed=2 * 10**6, transcendentals=0),
        name=name,
    )


def some_rows(rows_ref, tile, count):
    return jnp.concatenate([rows_ref[t : t + 1, :] for t in range(tile, tile + count)], axis=1)


def one_hot(rows):
    line = lax.broadcasted_iota(jnp.int32, (LANES, rows.shape[1]), 0).astype(F32).astype(BF16)
    column = (rows % LANES).astype(F32).astype(BF16)
    return jnp.where(column == line, jnp.ones((), BF16), jnp.zeros((), BF16))


def scattered(rows_ref, back_ref, chunks):
    tiles, width = rows_ref.shape
    zero = jnp.zeros((), BF16)
    total = None
    for start in range(0, tiles, GROUP):
        rows = some_rows(rows_ref, start, GROUP)
        chunk = (rows // LANES).astype(F32).astype(BF16)
        back = back_ref[:, start * width : (start + GROUP) * width]
        spread = jnp.concatenate([jnp.where(chunk == k, back, zero) for k in chunks], axis=0)
        part = lax.dot_general(
            spread, one_hot(rows), (((1,), (1,)), ((), ())), preferred_element_type=F32
        )
        total = part if total is None else total + part
    return total.astype(BF16)


def back_kernel(
    live_hbm, cot_hbm, weights_hbm, back_ref, kept_ref, live_ref, cot_ref, weights_ref, sems
):
    tiles, width, _ = weights_ref.shape
    copies = [
        pltpu.make_async_copy(live_hbm, live_ref, sems.at[0]),
        pltpu.make_async_copy(cot_hbm, cot_ref, sems.at[1]),
    ]
    starts = range(0, tiles, GROUP)
    for i, start in enumerate(starts):
        at = pl.ds(start, GROUP)
        copies.append(pltpu.make_async_copy(weights_hbm.at[at], weights_ref.at[at], sems.at[2 + i]))
    for copy in copies:
        copy.start()
    copies[0].wait()
    first = lax.axis_index("mem") * tiles
    live = live_ref[0, 0]
    kept_ref[...] = jnp.full(kept_ref.shape, live - first, jnp.int32)
    copies[1].wait()
    for i, start in enumerate(starts):
        copies[2 + i].wait()
        for tile in range(start, start + GROUP):
            at = slice(tile * width, (tile + 1) * width)
            back = lax.dot_general(
                weights_ref[tile], cot_ref[:, at], (((1,), (1,)), ((), ())), preferred_element_type=F32
            ).T
            back_ref[:, at] = jnp.where(first + tile < live, back, 0.0).astype(BF16)


def back_blocks(live, cot, weights):
    hbm = pl.BlockSpec(memory_space=pltpu.HBM)
    out = (
        jax.ShapeDtypeStruct(cot.shape, BF16),
        jax.ShapeDtypeStruct((8, weights.shape[2]), jnp.int32),
    )
    live = live.reshape(1, 1)
    scratch = [
        pltpu.SMEM(live.shape, live.dtype),
        pltpu.VMEM(cot.shape, cot.dtype),
        pltpu.VMEM(weights.shape, weights.dtype),
        pltpu.SemaphoreType.DMA((2 + weights.shape[0] // GROUP,)),
    ]
    return compiled(back_kernel, out, [hbm] * 3, "back_blocks", scratch, mib=53.55)(live, cot, weights)


def sides_kernel(rows_ref, back_ref, out_ref):
    out_ref[...] = scattered(rows_ref, back_ref, SIDES)


def sides_sums(rows, back):
    vmem = pl.BlockSpec(memory_space=pltpu.VMEM)
    out = jax.ShapeDtypeStruct((len(SIDES) * back.shape[0], LANES), BF16)
    return compiled(sides_kernel, out, [vmem, vmem], "sides_sums")(rows, back)


def inner_kernel(pert_ref, weights_ref, modes_ref, rows_ref, back_ref, out_ref):
    members, levels, points = pert_ref.shape
    for chunk in range(CHUNKS):
        at = slice(chunk * LANES, (chunk + 1) * LANES)
        total = jnp.zeros((levels, LANES), F32)
        for k in range(members):
            alpha = lax.dot_general(
                modes_ref[...],
                weights_ref[k, :, at],
                (((0,), (0,)), ((), ())),
                preferred_element_type=F32,
            )
            total = total + pert_ref[k, :, at].astype(F32) * alpha
        out_ref[chunk * levels : (chunk + 1) * levels, :] = total.astype(BF16)
    out_ref[CHUNKS * levels :, :] = scattered(rows_ref, back_ref, CENTRE)


def inner_sums(pert, mode_weights, modes, rows, back):
    vmem = pl.BlockSpec(memory_space=pltpu.VMEM)
    out = jax.ShapeDtypeStruct((2 * CHUNKS * pert.shape[1], LANES), BF16)
    return compiled(inner_kernel, out, [vmem] * 5, "inner_sums")(pert, mode_weights, modes, rows, back)


def add(*refs):
    return functools.reduce(jnp.add, [ref.astype(F32) for ref in refs])


def outward_kernel(both_ref, out_ref):
    size = out_ref.shape[0]
    core = lax.axis_index("mem") % 2
    at = pl.ds(pl.multiple_of((1 - core) * size, size), size)
    out_ref[...] = add(both_ref[0, at, :], both_ref[1, at, :]).astype(BF16)


def outward(both):
    vmem = pl.BlockSpec(memory_space=pltpu.VMEM)
    out = jax.ShapeDtypeStruct((both.shape[1] // 2, LANES), BF16)
    return compiled(outward_kernel, out, [vmem], "outward", flops=10**6)(both)


def chip_kernel(inner_ref, came_ref, out_ref):
    size = came_ref.shape[1]
    half = size // 2
    core = lax.axis_index("mem") % 2
    here = pl.ds(pl.multiple_of(core * half, half), half)
    centre = pl.ds(pl.multiple_of(size + core * half, half), half)
    out_ref[:half, :] = add(inner_ref[0, here, :], inner_ref[1, here, :]).astype(BF16)
    out_ref[half:, :] = add(
        inner_ref[0, centre, :], inner_ref[1, centre, :], came_ref[0, here, :], came_ref[1, here, :]
    ).astype(BF16)


def chip_sums(inner, came):
    vmem = pl.BlockSpec(memory_space=pltpu.VMEM)
    out = jax.ShapeDtypeStruct(came.shape[1:], BF16)
    return compiled(chip_kernel, out, [vmem, vmem], "chip_sums", flops=10**6)(inner, came)


def total_kernel(parts_ref, out_ref):
    out_ref[...] = add(*[parts_ref[i] for i in range(parts_ref.shape[0])]).astype(BF16)


def totals(parts):
    vmem = pl.BlockSpec(memory_space=pltpu.VMEM)
    out = jax.ShapeDtypeStruct(parts.shape[1:], BF16)
    return compiled(total_kernel, out, [vmem], "totals", flops=10**6)(parts)


def middle_kernel(both_ref, out_ref):
    half = both_ref.shape[1] // 2
    out_ref[:half, :] = both_ref[0, :half, :]
    out_ref[half:, :] = both_ref[1, :half, :]


def middle_of(both):
    vmem = pl.BlockSpec(memory_space=pltpu.VMEM)
    out = jax.ShapeDtypeStruct(both.shape[1:], BF16)
    return compiled(middle_kernel, out, [vmem], "middle", flops=10**6)(both)


def pick(table, rows, block, chunks):
    levels = block.shape[0]
    picked = jnp.dot(table, one_hot(rows), preferred_element_type=F32)
    chunk = rows // LANES
    for i, k in enumerate(chunks):
        block = jnp.where(chunk == k, picked[i * levels : (i + 1) * levels], block)
    return block.astype(BF16)


def centre_kernel(rows_ref, middle_ref, out_ref):
    tiles, width = rows_ref.shape
    for tile in range(0, tiles, STEP):
        at = slice(tile * width, (tile + STEP) * width)
        none = jnp.zeros((out_ref.shape[0], STEP * width), F32)
        rows = some_rows(rows_ref, tile, STEP)
        out_ref[:, at] = pick(middle_ref[...], rows, none, CENTRE)


def centre_blocks(rows, middle):
    vmem = pl.BlockSpec(memory_space=pltpu.VMEM)
    out = jax.ShapeDtypeStruct((middle.shape[0] // CHUNKS, rows.size), BF16)
    return compiled(centre_kernel, out, [vmem, vmem], "centre_blocks")(rows, middle)


def fine_kernel(kept_ref, rows_ref, weights_ref, centre_ref, sides_ref, out_ref, block_ref):
    tiles, width, _ = weights_ref.shape
    kept = kept_ref[:1, :]
    sides = jnp.concatenate([sides_ref[0], sides_ref[1]], axis=0)
    for tile in range(0, tiles, STEP):
        at = slice(tile * width, (tile + STEP) * width)
        rows = some_rows(rows_ref, tile, STEP)
        block_ref[:, at] = pick(sides, rows, centre_ref[:, at].astype(F32), SIDES)
    for tile in range(tiles):
        at = slice(tile * width, (tile + 1) * width)
        fine = jnp.dot(block_ref[:, at], weights_ref[tile], preferred_element_type=F32)
        out_ref[:, at] = jnp.where(tile < kept, fine, 0.0).astype(BF16)


def fine_sum(kept, rows, weights, blocks, sides):
    vmem = pl.BlockSpec(memory_space=pltpu.VMEM)
    out = jax.ShapeDtypeStruct(blocks.shape, BF16)
    scratch = [pltpu.VMEM(blocks.shape, BF16)]
    return compiled(fine_kernel, out, [vmem] * 5, "fine_sum", scratch)(kept, rows, weights, blocks, sides)


def gradient_kernel(pert_ref, modes_ref, both_ref, out_ref):
    members, levels, points = pert_ref.shape
    half = both_ref.shape[1] // 2
    modes = jnp.concatenate([modes_ref[...], modes_ref[...]], axis=1)
    chunks = points // LANES
    for chunk in range(chunks):
        at = slice(chunk * LANES, (chunk + 1) * LANES)
        side, row = divmod(chunk * levels, half)
        adjoint = both_ref[side, half + row : half + row + levels, :].astype(F32)
        for k in range(members):
            product = pert_ref[k, :, at].astype(F32) * adjoint
            high = product.astype(BF16)
            low = (product - high.astype(F32)).astype(BF16)
            both = jnp.concatenate([high, low], axis=0)
            out_ref[k, :, at] = jnp.dot(modes, both, preferred_element_type=F32).astype(BF16)


def gradient(pert, modes, both):
    members, levels, points = pert.shape
    vmem = pl.BlockSpec(memory_space=pltpu.VMEM)
    out = jax.ShapeDtypeStruct((members, modes.shape[0], points), BF16)
    return compiled(gradient_kernel, out, [vmem, vmem, vmem], "gradient")(pert, modes, both)


def halo_route(bands, mems, near):
    route = []
    for b in range(bands):
        for m in range(mems):
            step = 1 - 2 * (m % 2)
            to = b + step
            if 0 <= to < bands:
                turn = 2 * step if to // near != b // near else 0
                route.append((b * mems + m, to * mems + (m + turn) % mems))
    return route


def shards(
    perturbations,
    mode_weights,
    vertical_modes,
    interp_weights,
    source_rows,
    live_tiles,
    fine_cotangent,
):
    bands, mems = lax.axis_size("band"), lax.axis_size("mem")
    pairs = [[m, m + 1] for m in range(0, mems, 2)]
    chips = [list(range(c, mems, 2)) for c in range(2)]
    to_pair = functools.partial(lax.all_gather, axis_name="mem", axis_index_groups=pairs)
    to_chips = functools.partial(lax.all_gather, axis_name="mem", axis_index_groups=chips)
    to_bands = functools.partial(
        lax.ppermute, axis_name=("band", "mem"), perm=halo_route(bands, mems, NEAR)
    )

    modes = vertical_modes.T
    back, kept = back_blocks(live_tiles, fine_cotangent, interp_weights)
    came = to_bands(outward(to_pair(sides_sums(source_rows, back))))
    inner = to_pair(inner_sums(perturbations, mode_weights, modes, source_rows, back))
    sums = totals(to_chips(chip_sums(inner, to_pair(came))))
    both = to_pair(sums)
    middle = middle_of(both)
    came = to_bands(middle)
    mode_gradient = gradient(perturbations, modes, both)
    blocks = centre_blocks(source_rows, middle)
    fine_increment = fine_sum(kept, source_rows, interp_weights, blocks, to_pair(came))
    return (fine_increment, mode_gradient)


def solution(mesh):
    placed = (
        P("mem", None, "band"),
        P("mem", None, "band"),
        P(),
        P(("band", "mem"), None, None),
        P(("band", "mem"), None),
        P("band"),
        P(None, ("band", "mem")),
    )
    return jax.shard_map(
        shards,
        mesh=mesh,
        in_specs=placed,
        out_specs=(P(None, ("band", "mem")), P("mem", None, "band")),
        check_vma=False,
    )
```

time: 192 us -> 71.1 us (0.37)
  waiting for transfers between devices: 50.9 us -> 0.01 us
  local copies, waits for them, and re-layouts: 26.1 us -> 0.03 us
  other arithmetic: 25.9 us -> 0 us
  between operations: 14.9 us -> 1.41 us
  blocking collectives: 49 us -> 39.2 us
  Pallas kernels: 0 us -> 9.43 us
  matrix products: 5.76 us -> 0 us
    psum x1 -> x0, waiting for transfers between devices: 50.8 us -> none  [shards(): summed = lax.psum(local_adj, 'mem')]
    psum x1 -> x0, blocking collectives: 49 us -> none  [shards(): total = lax.psum(partial_sum, 'mem')]
    all_gather x0 -> x6, blocking collectives: none -> 39.2 us  [the longest x2 28.3 us: shards(): sums = totals(to_chips(chip_sums(inner, to_pair(came))))]
    scatter-add x1 -> x0, other arithmetic: 24.2 us -> none  [shards(): local_adj = jnp.zeros((levels, 3 * grid_points), jnp.float32).at[:, sourc...]
    gather x2 -> x0, local copies, waits for them, and re-layouts: 16.6 us -> none  [shards(): block = jnp.take(extended, source_rows, axis=1)]
    pallas_call x0 -> x10, Pallas kernels: none -> 9.43 us  [the longest x1 2.24 us: fine_sum(): compiled(fine_kernel, out, [vmem] * 5, 'fine_sum', scratch)]
    dot_general x4 -> x0, matrix products: 5.76 us -> none  [the longest x1 2.09 us: shards(): jnp.einsum('lm,klp->kmp', vertical_modes.astype(jnp.float32), product, pr...]
    reshape x3 -> x0, local copies, waits for them, and re-layouts: 3.24 us -> none  [the longest x2 2.48 us: shards(): back.reshape(levels, -1)]
  transfers between devices with their start and end apart: 5 -> 2, of which waited for: 1 -> 0; matrix products, arithmetic and copies ran while one was open for 12% -> 0% of each run, Pallas kernels for 0% -> 5%
where the time goes in v2:
time: 71.1 us; the launch traced here: 70.9 us
  blocking collectives  39.2 us (55%)
  starting transfers between devices  20.8 us (29%)
  Pallas kernels  9.43 us (13%)
  between operations  1.41 us (2%)
    all_gather x2, blocking collectives, shards(): sums = totals(to_chips(chip_sums(inner, to_pair(came))))  28.3 us
    ppermute x1, starting transfers between devices, shards(): came = to_bands(outward(to_pair(sides_sums(source_rows, back))))  13.8 us
    ppermute x1, starting transfers between devices, shards(): came = to_bands(middle)  6.93 us
    all_gather x1, blocking collectives, shards(): to_pair(came)  3.92 us
    all_gather x1, blocking collectives, shards(): came = to_bands(outward(to_pair(sides_sums(source_rows, back))))  2.61 us
    pallas_call x1, Pallas kernels, fine_sum(): compiled(fine_kernel, out, [vmem] * 5, 'fine_sum', scratch)  2.24 us
    all_gather x1, blocking collectives, shards(): both = to_pair(sums)  2.21 us
    all_gather x1, blocking collectives, shards(): to_pair(inner_sums(perturbations, mode_weights, modes, source_rows, back))  2.18 us
  transfers between devices with their start and end apart: 2, of which 0 were waited for; matrix products, arithmetic and copies ran while one was open for 0% of the time, Pallas kernels for 5%

profile of v2, /device:TPU:7, one launch (start us, length us, event | category | flops | bytes accessed | tf_op | source)
XLA Modules:
  0.0 70.9 jit_solution(4482586713384940863)
XLA Ops:
  1.3 0.0 copy-start.3
  1.3 2.2 %back_blocks.1 = (bf16[32,4096]{1,0:T(8,128)(2,1)S(1)}, s32[8,128]{1,0:T(8,128)S(1)}) custom-call(s32[1,1]{1,0:T(1,128)} %bitcast.8.live_hbm, bf16[32,4096]{1,0:T(8,128)(2,1)} %cot_hbm.1, bf16[32,128,128]{2,1,0:T(8,128)(2,1)} %weights_ref.3), custom_call_target="tpu_custom_call" | custom-call | flops 2000000000 | bytes 2000000 | tf_op jit(solution)/shard_map/back_blocks/pallas_call | solution.py:105
  3.5 0.0 copy-done.3
  3.5 0.0 copy-start.2
  3.5 1.3 %sides_sums.1 = bf16[512,256]{1,0:T(8,128)(2,1)S(1)} custom-call(s32[32,128]{1,0:T(8,128)S(1)} %copy-done.3, bf16[32,4096]{1,0:T(8,128)(2,1)S(1)} %get-tuple-element.5.back_ref), custom_call_target="tpu_custom_call" | custom-call | flops 2000000000 | bytes 2000000 | tf_op jit(solution)/shard_map/sides_sums/pallas_call | solution.py:115
  4.8 0.0 copy-start
  4.8 0.0 copy-start.4
  4.8 2.6 %all-gather.1 = bf16[1024,256]{1,0:T(8,128)(2,1)S(1)} all-gather(bf16[512,256]{1,0:T(8,128)(2,1)S(1)} %sides_sums.1), channel_id=3, replica_groups={{0,1},{2,3},{4,5},{6,7},{8,9},{10,11},{12,13},{14,15},{16,17},{18,19},{..., dimensions={0}, use_global_device_ids=true | all-gather | bytes 786432 | tf_op jit(solution)/shard_map/all_gather | solution.py:299
  7.5 13.8 %collective-permute-start = (bf16[256,256]{1,0:T(8,128)(2,1)S(1)}, bf16[256,256]{1,0:T(8,128)(2,1)S(1)}, u32[]{:S(2)}, u32[]{:S(2)}) collective-permute-start(bf16[256,256]{1,0:T(8,128)(2,1)S(1)} %outward.1), channel_id=1, source_target_pairs={{0,8},{2,10},{4,12},{6,14},{8,16},{9,1},{10,18},{11,3},{12,20},{13... | collective-permute-start | bytes 393224 | tf_op jit(solution)/shard_map/ppermute | solution.py:299
  21.3 0.0 copy-done.2
  21.3 0.0 copy-done
  21.3 0.0 copy-done.4
  21.3 1.4 %inner_sums.1 = bf16[512,256]{1,0:T(8,128)(2,1)S(1)} custom-call(bf16[10,32,2048]{2,1,0:T(8,128)(2,1)S(1)} %copy-done, bf16[10,16,2048]{2,1,0:T(8,128)(2,1)S(1)} %copy-done.2, bf16[16,32]{1,0:T(8,128)(2,1)S(1)} %bitcast.16, s32[32,128]{1,0:T(8,128)S(1)} %copy-done.3, bf16[32,4096]{1,0:T(8,128)(2,1)S(1)} %get-tuple-element.5.back_ref), custom_call_target="tpu_custom_call" | custom-call | flops 2000000000 | bytes 2000000 | tf_op jit(solution)/shard_map/inner_sums/pallas_call | solution.py:138
  22.7 2.2 %all-gather = bf16[1024,256]{1,0:T(8,128)(2,1)S(1)} all-gather(bf16[512,256]{1,0:T(8,128)(2,1)S(1)} %inner_sums.1), channel_id=2, replica_groups={{0,1},{2,3},{4,5},{6,7},{8,9},{10,11},{12,13},{14,15},{16,17},{18,19},{..., dimensions={0}, use_global_device_ids=true | all-gather | bytes 786432 | tf_op jit(solution)/shard_map/all_gather | solution.py:300
  24.9 0.0 collective-permute-done
  24.9 2.0 %all-gather.2 = bf16[512,256]{1,0:T(8,128)(2,1)S(1)} all-gather(bf16[256,256]{1,0:T(8,128)(2,1)S(1)} %collective-permute-done), channel_id=4, replica_groups={{0,1},{2,3},{4,5},{6,7},{8,9},{10,11},{12,13},{14,15},{16,17},{18,19},{..., dimensions={0}, use_global_device_ids=true | all-gather | bytes 393216 | tf_op jit(solution)/shard_map/all_gather | solution.py:301
  26.9 0.1 chip_sums.1
  26.9 26.3 %all-gather.3 = bf16[1024,256]{1,0:T(8,128)(2,1)S(1)} all-gather(bf16[256,256]{1,0:T(8,128)(2,1)S(1)} %chip_sums.1), channel_id=5, replica_groups={{0,2,4,6},{1,3,5,7},{8,10,12,14},{9,11,13,15},{16,18,20,22},{17,19,21,2..., dimensions={0}, use_global_device_ids=true | all-gather | bytes 655360 | tf_op jit(solution)/shard_map/all_gather | solution.py:301
  53.3 0.1 totals.1
  53.3 2.2 %all-gather.4 = bf16[512,256]{1,0:T(8,128)(2,1)S(1)} all-gather(bf16[256,256]{1,0:T(8,128)(2,1)S(1)} %totals.1), channel_id=6, replica_groups={{0,1},{2,3},{4,5},{6,7},{8,9},{10,11},{12,13},{14,15},{16,17},{18,19},{..., dimensions={0}, use_global_device_ids=true | all-gather | bytes 393216 | tf_op jit(solution)/shard_map/all_gather | solution.py:302
  55.5 6.9 %collective-permute-start.1 = (bf16[256,256]{1,0:T(8,128)(2,1)S(1)}, bf16[256,256]{1,0:T(8,128)(2,1)S(1)}, u32[]{:S(2)}, u32[]{:S(2)}) collective-permute-start(bf16[256,256]{1,0:T(8,128)(2,1)S(1)} %middle.1.middle_ref), channel_id=1, source_target_pairs={{0,8},{2,10},{4,12},{6,14},{8,16},{9,1},{10,18},{11,3},{12,20},{13... | collective-permute-start | bytes 393224 | tf_op jit(solution)/shard_map/ppermute | solution.py:304
  62.5 0.7 %centre_blocks.1.centre_ref = bf16[32,4096]{1,0:T(8,128)(2,1)S(1)} custom-call(s32[32,128]{1,0:T(8,128)S(1)} %copy-done.3, bf16[256,256]{1,0:T(8,128)(2,1)S(1)} %middle.1.middle_ref), custom_call_target="tpu_custom_call" | custom-call | flops 2000000000 | bytes 2000000 | tf_op jit(solution)/shard_map/centre_blocks/pallas_call | solution.py:219
  63.2 0.0 copy-start.1
  63.2 1.4 %gradient.1 = bf16[10,16,2048]{2,1,0:T(8,128)(2,1)} custom-call(bf16[10,32,2048]{2,1,0:T(8,128)(2,1)S(1)} %copy-done, bf16[16,32]{1,0:T(8,128)(2,1)S(1)} %bitcast.17, bf16[2,256,256]{2,1,0:T(8,128)(2,1)S(1)} %bitcast.14), custom_call_target="tpu_custom_call" | custom-call | flops 2000000000 | bytes 2000000 | tf_op jit(solution)/shard_map/gradient/pallas_call | solution.py:264
  64.7 0.0 collective-permute-done.1
  64.7 3.9 %all-gather.5 = bf16[512,256]{1,0:T(8,128)(2,1)S(1)} all-gather(bf16[256,256]{1,0:T(8,128)(2,1)S(1)} %collective-permute-done.1), channel_id=7, replica_groups={{0,1},{2,3},{4,5},{6,7},{8,9},{10,11},{12,13},{14,15},{16,17},{18,19},{..., dimensions={0}, use_global_device_ids=true | all-gather | bytes 393216 | tf_op jit(solution)/shard_map/all_gather | solution.py:307
  68.6 0.0 copy-done.1
  68.6 2.2 %fine_sum.1 = bf16[32,4096]{1,0:T(8,128)(2,1)} custom-call(s32[8,128]{1,0:T(8,128)S(1)} %get-tuple-element.4.kept_ref, s32[32,128]{1,0:T(8,128)S(1)} %copy-done.3, bf16[32,128,128]{2,1,0:T(8,128)(2,1)S(1)} %copy-done.1, bf16[32,4096]{1,0:T(8,128)(2,1)S(1)} %centre_blocks.1.centre_ref, bf16[2,256,256]{2,1,0:T(8,128)(2,1)S(1)} %bitcast.15), custom_call_target="tpu_custom_call" | custom-call | flops 2000000000 | bytes 2000000 | tf_op jit(solution)/shard_map/fine_sum/pallas_call | solution.py:240
  (2 shorter events, 0.0 us)
Async XLA Ops:
  1.3 2.2 %copy-start.3 = (s32[32,128]{1,0:T(8,128)S(1)}, s32[32,128]{1,0:T(8,128)}, u32[]{:S(2)}) copy-start(s32[32,128]{1,0:T(8,128)} %rows_ref.7) | copy-start | bytes 49156
  3.5 17.8 %copy-start.2 = (bf16[10,16,2048]{2,1,0:T(8,128)(2,1)S(1)}, bf16[10,16,2048]{2,1,0:T(8,128)(2,1)}, u32[]{:S(2)}) copy-start(bf16[10,16,2048]{2,1,0:T(8,128)(2,1)} %weights_ref.2) | copy-start | bytes 1966084
  4.8 16.5 %copy-start = (bf16[10,32,2048]{2,1,0:T(8,128)(2,1)S(1)}, bf16[10,32,2048]{2,1,0:T(8,128)(2,1)}, u32[]{:S(2)}) copy-start(bf16[10,32,2048]{2,1,0:T(8,128)(2,1)} %pert_ref.3) | copy-start | bytes 3932164
  4.8 16.5 %copy-start.4 = (bf16[32,16]{0,1:T(8,128)(2,1)S(1)}, bf16[32,16]{0,1:T(8,128)(2,1)}, u32[]{:S(2)}) copy-start(bf16[32,16]{0,1:T(8,128)(2,1)} %param.9) | copy-start | bytes 3076
  7.5 17.4 %collective-permute-start = (bf16[256,256]{1,0:T(8,128)(2,1)S(1)}, bf16[256,256]{1,0:T(8,128)(2,1)S(1)}, u32[]{:S(2)}, u32[]{:S(2)}) collective-permute-start(bf16[256,256]{1,0:T(8,128)(2,1)S(1)} %outward.1), channel_id=1, source_target_pairs={{0,8},{2,10},{4,12},{6,14},{8,16},{9,1},{10,18},{11,3},{12,20},{13... | collective-permute-start | bytes 393224 | tf_op jit(solution)/shard_map/ppermute | solution.py:299
  55.5 9.1 %collective-permute-start.1 = (bf16[256,256]{1,0:T(8,128)(2,1)S(1)}, bf16[256,256]{1,0:T(8,128)(2,1)S(1)}, u32[]{:S(2)}, u32[]{:S(2)}) collective-permute-start(bf16[256,256]{1,0:T(8,128)(2,1)S(1)} %middle.1.middle_ref), channel_id=1, source_target_pairs={{0,8},{2,10},{4,12},{6,14},{8,16},{9,1},{10,18},{11,3},{12,20},{13... | collective-permute-start | bytes 393224 | tf_op jit(solution)/shard_map/ppermute | solution.py:304
  63.2 5.4 %copy-start.1 = (bf16[32,128,128]{2,1,0:T(8,128)(2,1)S(1)}, bf16[32,128,128]{2,1,0:T(8,128)(2,1)}, u32[]{:S(2)}) copy-start(bf16[32,128,128]{2,1,0:T(8,128)(2,1)} %weights_ref.3) | copy-start | bytes 3145732

commit v3 on v2

--- a/solution.py
+++ b/solution.py
@@ -57,7 +57,7 @@
             spread, one_hot(rows), (((1,), (1,)), ((), ())), preferred_element_type=F32
         )
         total = part if total is None else total + part
-    return total.astype(BF16)
+    return total
 
 
 def back_kernel(
@@ -106,7 +106,7 @@
 
 
 def sides_kernel(rows_ref, back_ref, out_ref):
-    out_ref[...] = scattered(rows_ref, back_ref, SIDES)
+    out_ref[...] = scattered(rows_ref, back_ref, SIDES).astype(BF16)
 
 
 def sides_sums(rows, back):
@@ -115,7 +115,7 @@
     return compiled(sides_kernel, out, [vmem, vmem], "sides_sums")(rows, back)
 
 
-def inner_kernel(pert_ref, weights_ref, modes_ref, rows_ref, back_ref, out_ref):
+def inner_kernel(pert_ref, weights_ref, modes_ref, rows_ref, back_ref, out_ref, own_ref):
     members, levels, points = pert_ref.shape
     for chunk in range(CHUNKS):
         at = slice(chunk * LANES, (chunk + 1) * LANES)
@@ -128,13 +128,15 @@
                 preferred_element_type=F32,
             )
             total = total + pert_ref[k, :, at].astype(F32) * alpha
-        out_ref[chunk * levels : (chunk + 1) * levels, :] = total.astype(BF16)
-    out_ref[CHUNKS * levels :, :] = scattered(rows_ref, back_ref, CENTRE)
+        own_ref[chunk * levels : (chunk + 1) * levels, :] = total
+    own_ref[CHUNKS * levels :, :] = scattered(rows_ref, back_ref, CENTRE)
+    out_ref[...] = own_ref[...].astype(BF16)
 
 
 def inner_sums(pert, mode_weights, modes, rows, back):
     vmem = pl.BlockSpec(memory_space=pltpu.VMEM)
-    out = jax.ShapeDtypeStruct((2 * CHUNKS * pert.shape[1], LANES), BF16)
+    shape = (2 * CHUNKS * pert.shape[1], LANES)
+    out = (jax.ShapeDtypeStruct(shape, BF16), jax.ShapeDtypeStruct(shape, F32))
     return compiled(inner_kernel, out, [vmem] * 5, "inner_sums")(pert, mode_weights, modes, rows, back)
 
 
@@ -155,32 +157,40 @@
     return compiled(outward_kernel, out, [vmem], "outward", flops=10**6)(both)
 
 
-def chip_kernel(inner_ref, came_ref, out_ref):
+def chip_kernel(inner_ref, own_ref, came_ref, out_ref, exact_ref):
     size = came_ref.shape[1]
     half = size // 2
     core = lax.axis_index("mem") % 2
     here = pl.ds(pl.multiple_of(core * half, half), half)
     centre = pl.ds(pl.multiple_of(size + core * half, half), half)
-    out_ref[:half, :] = add(inner_ref[0, here, :], inner_ref[1, here, :]).astype(BF16)
-    out_ref[half:, :] = add(
-        inner_ref[0, centre, :], inner_ref[1, centre, :], came_ref[0, here, :], came_ref[1, here, :]
-    ).astype(BF16)
-
-
-def chip_sums(inner, came):
-    vmem = pl.BlockSpec(memory_space=pltpu.VMEM)
-    out = jax.ShapeDtypeStruct(came.shape[1:], BF16)
-    return compiled(chip_kernel, out, [vmem, vmem], "chip_sums", flops=10**6)(inner, came)
-
-
-def total_kernel(parts_ref, out_ref):
-    out_ref[...] = add(*[parts_ref[i] for i in range(parts_ref.shape[0])]).astype(BF16)
-
-
-def totals(parts):
-    vmem = pl.BlockSpec(memory_space=pltpu.VMEM)
-    out = jax.ShapeDtypeStruct(parts.shape[1:], BF16)
-    return compiled(total_kernel, out, [vmem], "totals", flops=10**6)(parts)
+    exact_ref[:half, :] = add(own_ref[here, :], inner_ref[1 - core, here, :])
+    exact_ref[half:, :] = add(
+        own_ref[centre, :], inner_ref[1 - core, centre, :], came_ref[0, here, :], came_ref[1, here, :]
+    )
+    out_ref[...] = exact_ref[...].astype(BF16)
+
+
+def chip_sums(inner, own, came):
+    vmem = pl.BlockSpec(memory_space=pltpu.VMEM)
+    shape = came.shape[1:]
+    out = (jax.ShapeDtypeStruct(shape, BF16), jax.ShapeDtypeStruct(shape, F32))
+    return compiled(chip_kernel, out, [vmem] * 3, "chip_sums", flops=10**6)(inner, own, came)
+
+
+def join_kernel(step, parts_ref, own_ref, out_ref, *exact_ref):
+    mem = lax.axis_index("mem")
+    other = 1 - (mem // 2 + mem % 2 + step) % 2
+    total = own_ref[...] + parts_ref[other].astype(F32)
+    out_ref[...] = total.astype(BF16)
+    if exact_ref:
+        exact_ref[0][...] = total
+
+
+def join(step, parts, own):
+    vmem = pl.BlockSpec(memory_space=pltpu.VMEM)
+    out = [jax.ShapeDtypeStruct(own.shape, BF16), jax.ShapeDtypeStruct(own.shape, F32)][: 2 - step]
+    kernel = functools.partial(join_kernel, step)
+    return compiled(kernel, out, [vmem, vmem], "join", flops=10**6)(parts, own)
 
 
 def middle_kernel(both_ref, out_ref):
@@ -276,6 +286,16 @@
     return route
 
 
+def chip_pairs(mems, step):
+    chips = mems // 2
+    return [
+        [2 * chip + core, 2 * ((chip + 1) % chips) + core]
+        for core in range(2)
+        for chip in range(chips)
+        if (chip + core + step) % 2 == 0
+    ]
+
+
 def shards(
     perturbations,
     mode_weights,
@@ -287,9 +307,7 @@
 ):
     bands, mems = lax.axis_size("band"), lax.axis_size("mem")
     pairs = [[m, m + 1] for m in range(0, mems, 2)]
-    chips = [list(range(c, mems, 2)) for c in range(2)]
     to_pair = functools.partial(lax.all_gather, axis_name="mem", axis_index_groups=pairs)
-    to_chips = functools.partial(lax.all_gather, axis_name="mem", axis_index_groups=chips)
     to_bands = functools.partial(
         lax.ppermute, axis_name=("band", "mem"), perm=halo_route(bands, mems, NEAR)
     )
@@ -297,8 +315,12 @@
     modes = vertical_modes.T
     back, kept = back_blocks(live_tiles, fine_cotangent, interp_weights)
     came = to_bands(outward(to_pair(sides_sums(source_rows, back))))
-    inner = to_pair(inner_sums(perturbations, mode_weights, modes, source_rows, back))
-    sums = totals(to_chips(chip_sums(inner, to_pair(came))))
+    inner, own = inner_sums(perturbations, mode_weights, modes, source_rows, back)
+    sums, own = chip_sums(to_pair(inner), own, to_pair(came))
+    for step in range(2):
+        parts = lax.all_gather(sums, "mem", axis_index_groups=chip_pairs(mems, step))
+        sums, *own = join(step, parts, own)
+        own = own[0] if own else None
     both = to_pair(sums)
     middle = middle_of(both)
     came = to_bands(middle)

time: 71.1 us -> 65.2 us (0.917)
  blocking collectives: 39.2 us -> 35.1 us
  starting transfers between devices: 20.8 us -> 19 us
    all_gather x3 -> x4, blocking collectives: 30.5 us -> 24.9 us  [the longest x2 20.7 us: shards(): lax.all_gather(sums, 'mem', axis_index_groups=chip_pairs(mems, step))]
    ppermute x1, starting transfers between devices: 6.93 us -> 5.15 us  [shards(): came = to_bands(middle)]
    all_gather x1, blocking collectives: 3.92 us -> 5.63 us  [shards(): to_pair(came)]
where the time goes in v3:
time: 65.2 us; the launch traced here: 65 us
  blocking collectives  35.1 us (54%)
  starting transfers between devices  19 us (29%)
  Pallas kernels  9.44 us (14%)
  between operations  1.41 us (2%)
    all_gather x2, blocking collectives, shards(): lax.all_gather(sums, 'mem', axis_index_groups=chip_pairs(mems, step))  20.7 us
    ppermute x1, starting transfers between devices, shards(): came = to_bands(outward(to_pair(sides_sums(source_rows, back))))  13.8 us
    all_gather x1, blocking collectives, shards(): to_pair(came)  5.63 us
    ppermute x1, starting transfers between devices, shards(): came = to_bands(middle)  5.15 us
    all_gather x2, blocking collectives, shards(): sums, own = chip_sums(to_pair(inner), own, to_pair(came))  4.16 us
    all_gather x1, blocking collectives, shards(): came = to_bands(outward(to_pair(sides_sums(source_rows, back))))  2.61 us
    pallas_call x1, Pallas kernels, fine_sum(): compiled(fine_kernel, out, [vmem] * 5, 'fine_sum', scratch)  2.24 us
    pallas_call x1, Pallas kernels, back_blocks(): compiled(back_kernel, out, [hbm] * 3, 'back_blocks', scratch, mib=53.55)  2.17 us
  transfers between devices with their start and end apart: 2, of which 0 were waited for; matrix products, arithmetic and copies ran while one was open for 0% of the time, Pallas kernels for 5%

profile of v3, /device:TPU:7, one launch (start us, length us, event | category | flops | bytes accessed | tf_op | source)
XLA Modules:
  0.0 65.0 jit_solution(14385562878827579016)
XLA Ops:
  1.3 0.0 copy-start.3
  1.3 2.2 %back_blocks.1 = (bf16[32,4096]{1,0:T(8,128)(2,1)S(1)}, s32[8,128]{1,0:T(8,128)S(1)}) custom-call(s32[1,1]{1,0:T(1,128)} %bitcast.9.live_hbm, bf16[32,4096]{1,0:T(8,128)(2,1)} %cot_hbm.1, bf16[32,128,128]{2,1,0:T(8,128)(2,1)} %weights_ref.3), custom_call_target="tpu_custom_call" | custom-call | flops 2000000000 | bytes 2000000 | tf_op jit(solution)/shard_map/back_blocks/pallas_call | solution.py:105
  3.5 0.0 copy-done.3
  3.5 0.0 copy-start.2
  3.5 1.3 %sides_sums.1 = bf16[512,256]{1,0:T(8,128)(2,1)S(1)} custom-call(s32[32,128]{1,0:T(8,128)S(1)} %copy-done.3, bf16[32,4096]{1,0:T(8,128)(2,1)S(1)} %get-tuple-element.11.back_ref), custom_call_target="tpu_custom_call" | custom-call | flops 2000000000 | bytes 2000000 | tf_op jit(solution)/shard_map/sides_sums/pallas_call | solution.py:115
  4.8 0.0 copy-start
  4.8 0.0 copy-start.4
  4.8 2.6 %all-gather.1 = bf16[1024,256]{1,0:T(8,128)(2,1)S(1)} all-gather(bf16[512,256]{1,0:T(8,128)(2,1)S(1)} %sides_sums.1), channel_id=3, replica_groups={{0,1},{2,3},{4,5},{6,7},{8,9},{10,11},{12,13},{14,15},{16,17},{18,19},{..., dimensions={0}, use_global_device_ids=true | all-gather | bytes 786432 | tf_op jit(solution)/shard_map/all_gather | solution.py:317
  7.5 13.8 %collective-permute-start = (bf16[256,256]{1,0:T(8,128)(2,1)S(1)}, bf16[256,256]{1,0:T(8,128)(2,1)S(1)}, u32[]{:S(2)}, u32[]{:S(2)}) collective-permute-start(bf16[256,256]{1,0:T(8,128)(2,1)S(1)} %outward.1), channel_id=1, source_target_pairs={{0,8},{2,10},{4,12},{6,14},{8,16},{9,1},{10,18},{11,3},{12,20},{13... | collective-permute-start | bytes 393224 | tf_op jit(solution)/shard_map/ppermute | solution.py:317
  21.3 0.0 copy-done.2
  21.3 0.0 copy-done
  21.3 0.0 copy-done.4
  21.3 1.4 %inner_sums.1 = (bf16[512,256]{1,0:T(8,128)(2,1)S(1)}, f32[512,256]{1,0:T(8,128)S(1)}) custom-call(bf16[10,32,2048]{2,1,0:T(8,128)(2,1)S(1)} %copy-done, bf16[10,16,2048]{2,1,0:T(8,128)(2,1)S(1)} %copy-done.2, bf16[16,32]{1,0:T(8,128)(2,1)S(1)} %bitcast.18, s32[32,128]{1,0:T(8,128)S(1)} %copy-done.3, bf16[32,4096]{1,0:T(8,128)(2,1)S(1)} %get-tuple-element.11.back_ref), custom_call_target="tpu_custom_call" | custom-call | flops 2000000000 | bytes 2000000 | tf_op jit(solution)/shard_map/inner_sums/pallas_call | solution.py:140
  22.7 2.2 %all-gather = bf16[1024,256]{1,0:T(8,128)(2,1)S(1)} all-gather(bf16[512,256]{1,0:T(8,128)(2,1)S(1)} %get-tuple-element.12), channel_id=2, replica_groups={{0,1},{2,3},{4,5},{6,7},{8,9},{10,11},{12,13},{14,15},{16,17},{18,19},{..., dimensions={0}, use_global_device_ids=true | all-gather | bytes 786432 | tf_op jit(solution)/shard_map/all_gather | solution.py:319
  24.9 0.0 collective-permute-done
  24.9 2.0 %all-gather.2 = bf16[512,256]{1,0:T(8,128)(2,1)S(1)} all-gather(bf16[256,256]{1,0:T(8,128)(2,1)S(1)} %collective-permute-done), channel_id=4, replica_groups={{0,1},{2,3},{4,5},{6,7},{8,9},{10,11},{12,13},{14,15},{16,17},{18,19},{..., dimensions={0}, use_global_device_ids=true | all-gather | bytes 393216 | tf_op jit(solution)/shard_map/all_gather | solution.py:319
  26.9 0.1 chip_sums.1
  27.0 12.3 %all-gather.3 = bf16[512,256]{1,0:T(8,128)(2,1)S(1)} all-gather(bf16[256,256]{1,0:T(8,128)(2,1)S(1)} %get-tuple-element.14), channel_id=5, replica_groups={{0,2},{4,6},{3,5},{7,1},{8,10},{12,14},{11,13},{15,9},{16,18},{20,22},{..., dimensions={0}, use_global_device_ids=true | all-gather | bytes 393216 | tf_op jit(solution)/shard_map/all_gather | solution.py:321
  39.3 8.4 %all-gather.4 = bf16[512,256]{1,0:T(8,128)(2,1)S(1)} all-gather(bf16[256,256]{1,0:T(8,128)(2,1)S(1)} %get-tuple-element.16), channel_id=6, replica_groups={{2,4},{6,0},{1,3},{5,7},{10,12},{14,8},{9,11},{13,15},{18,20},{22,16},{..., dimensions={0}, use_global_device_ids=true | all-gather | bytes 393216 | tf_op jit(solution)/shard_map/all_gather | solution.py:321
  47.7 2.0 %all-gather.5 = bf16[512,256]{1,0:T(8,128)(2,1)S(1)} all-gather(bf16[256,256]{1,0:T(8,128)(2,1)S(1)} %join.3), channel_id=7, replica_groups={{0,1},{2,3},{4,5},{6,7},{8,9},{10,11},{12,13},{14,15},{16,17},{18,19},{..., dimensions={0}, use_global_device_ids=true | all-gather | bytes 393216 | tf_op jit(solution)/shard_map/all_gather | solution.py:324
  49.8 5.1 %collective-permute-start.1 = (bf16[256,256]{1,0:T(8,128)(2,1)S(1)}, bf16[256,256]{1,0:T(8,128)(2,1)S(1)}, u32[]{:S(2)}, u32[]{:S(2)}) collective-permute-start(bf16[256,256]{1,0:T(8,128)(2,1)S(1)} %middle.1.middle_ref), channel_id=1, source_target_pairs={{0,8},{2,10},{4,12},{6,14},{8,16},{9,1},{10,18},{11,3},{12,20},{13... | collective-permute-start | bytes 393224 | tf_op jit(solution)/shard_map/ppermute | solution.py:326
  54.9 0.7 %centre_blocks.1.centre_ref = bf16[32,4096]{1,0:T(8,128)(2,1)S(1)} custom-call(s32[32,128]{1,0:T(8,128)S(1)} %copy-done.3, bf16[256,256]{1,0:T(8,128)(2,1)S(1)} %middle.1.middle_ref), custom_call_target="tpu_custom_call" | custom-call | flops 2000000000 | bytes 2000000 | tf_op jit(solution)/shard_map/centre_blocks/pallas_call | solution.py:229
  55.7 0.0 copy-start.1
  55.7 1.4 %gradient.1 = bf16[10,16,2048]{2,1,0:T(8,128)(2,1)} custom-call(bf16[10,32,2048]{2,1,0:T(8,128)(2,1)S(1)} %copy-done, bf16[16,32]{1,0:T(8,128)(2,1)S(1)} %bitcast.19, bf16[2,256,256]{2,1,0:T(8,128)(2,1)S(1)} %bitcast.14), custom_call_target="tpu_custom_call" | custom-call | flops 2000000000 | bytes 2000000 | tf_op jit(solution)/shard_map/gradient/pallas_call | solution.py:274
  57.1 0.0 collective-permute-done.1
  57.1 5.6 %all-gather.6 = bf16[512,256]{1,0:T(8,128)(2,1)S(1)} all-gather(bf16[256,256]{1,0:T(8,128)(2,1)S(1)} %collective-permute-done.1), channel_id=8, replica_groups={{0,1},{2,3},{4,5},{6,7},{8,9},{10,11},{12,13},{14,15},{16,17},{18,19},{..., dimensions={0}, use_global_device_ids=true | all-gather | bytes 393216 | tf_op jit(solution)/shard_map/all_gather | solution.py:329
  62.7 0.0 copy-done.1
  62.7 2.2 %fine_sum.1 = bf16[32,4096]{1,0:T(8,128)(2,1)} custom-call(s32[8,128]{1,0:T(8,128)S(1)} %get-tuple-element.10.kept_ref, s32[32,128]{1,0:T(8,128)S(1)} %copy-done.3, bf16[32,128,128]{2,1,0:T(8,128)(2,1)S(1)} %copy-done.1, bf16[32,4096]{1,0:T(8,128)(2,1)S(1)} %centre_blocks.1.centre_ref, bf16[2,256,256]{2,1,0:T(8,128)(2,1)S(1)} %bitcast.17), custom_call_target="tpu_custom_call" | custom-call | flops 2000000000 | bytes 2000000 | tf_op jit(solution)/shard_map/fine_sum/pallas_call | solution.py:250
  (4 shorter events, 0.1 us)
Async XLA Ops:
  1.3 2.2 %copy-start.3 = (s32[32,128]{1,0:T(8,128)S(1)}, s32[32,128]{1,0:T(8,128)}, u32[]{:S(2)}) copy-start(s32[32,128]{1,0:T(8,128)} %rows_ref.7) | copy-start | bytes 49156
  3.5 17.8 %copy-start.2 = (bf16[10,16,2048]{2,1,0:T(8,128)(2,1)S(1)}, bf16[10,16,2048]{2,1,0:T(8,128)(2,1)}, u32[]{:S(2)}) copy-start(bf16[10,16,2048]{2,1,0:T(8,128)(2,1)} %weights_ref.2) | copy-start | bytes 1966084
  4.8 16.5 %copy-start = (bf16[10,32,2048]{2,1,0:T(8,128)(2,1)S(1)}, bf16[10,32,2048]{2,1,0:T(8,128)(2,1)}, u32[]{:S(2)}) copy-start(bf16[10,32,2048]{2,1,0:T(8,128)(2,1)} %pert_ref.3) | copy-start | bytes 3932164
  4.8 16.5 %copy-start.4 = (bf16[32,16]{0,1:T(8,128)(2,1)S(1)}, bf16[32,16]{0,1:T(8,128)(2,1)}, u32[]{:S(2)}) copy-start(bf16[32,16]{0,1:T(8,128)(2,1)} %param.9) | copy-start | bytes 3076
  7.5 17.4 %collective-permute-start = (bf16[256,256]{1,0:T(8,128)(2,1)S(1)}, bf16[256,256]{1,0:T(8,128)(2,1)S(1)}, u32[]{:S(2)}, u32[]{:S(2)}) collective-permute-start(bf16[256,256]{1,0:T(8,128)(2,1)S(1)} %outward.1), channel_id=1, source_target_pairs={{0,8},{2,10},{4,12},{6,14},{8,16},{9,1},{10,18},{11,3},{12,20},{13... | collective-permute-start | bytes 393224 | tf_op jit(solution)/shard_map/ppermute | solution.py:317
  49.8 7.4 %collective-permute-start.1 = (bf16[256,256]{1,0:T(8,128)(2,1)S(1)}, bf16[256,256]{1,0:T(8,128)(2,1)S(1)}, u32[]{:S(2)}, u32[]{:S(2)}) collective-permute-start(bf16[256,256]{1,0:T(8,128)(2,1)S(1)} %middle.1.middle_ref), channel_id=1, source_target_pairs={{0,8},{2,10},{4,12},{6,14},{8,16},{9,1},{10,18},{11,3},{12,20},{13... | collective-permute-start | bytes 393224 | tf_op jit(solution)/shard_map/ppermute | solution.py:326
  55.7 7.1 %copy-start.1 = (bf16[32,128,128]{2,1,0:T(8,128)(2,1)S(1)}, bf16[32,128,128]{2,1,0:T(8,128)(2,1)}, u32[]{:S(2)}) copy-start(bf16[32,128,128]{2,1,0:T(8,128)(2,1)} %weights_ref.3) | copy-start | bytes 3145732

commit v4 on v3

--- a/solution.py
+++ b/solution.py
@@ -20,13 +20,13 @@
 SIDES = [*range(CHUNKS), *range(2 * CHUNKS, 3 * CHUNKS)]
 
 
-def compiled(kernel, out, in_specs, name, scratch=(), flops=2 * 10**9, mib=32):
+def compiled(kernel, out, in_specs, name, scratch=(), flops=2 * 10**9, mib=32, out_spec=None):
     vmem = pl.BlockSpec(memory_space=pltpu.VMEM)
     return pl.pallas_call(
         kernel,
         out_shape=out,
         in_specs=in_specs,
-        out_specs=jax.tree.map(lambda _: vmem, out),
+        out_specs=jax.tree.map(lambda _: out_spec or vmem, out),
         scratch_shapes=list(scratch),
         compiler_params=pltpu.CompilerParams(vmem_limit_bytes=int(mib * 2**20)),
         cost_estimate=pl.CostEstimate(flops=flops, bytes_accessed=2 * 10**6, transcendentals=0),
@@ -67,26 +67,22 @@
     copies = [
         pltpu.make_async_copy(live_hbm, live_ref, sems.at[0]),
         pltpu.make_async_copy(cot_hbm, cot_ref, sems.at[1]),
+        pltpu.make_async_copy(weights_hbm, weights_ref, sems.at[2]),
     ]
-    starts = range(0, tiles, GROUP)
-    for i, start in enumerate(starts):
-        at = pl.ds(start, GROUP)
-        copies.append(pltpu.make_async_copy(weights_hbm.at[at], weights_ref.at[at], sems.at[2 + i]))
     for copy in copies:
         copy.start()
     copies[0].wait()
     first = lax.axis_index("mem") * tiles
     live = live_ref[0, 0]
     kept_ref[...] = jnp.full(kept_ref.shape, live - first, jnp.int32)
-    copies[1].wait()
-    for i, start in enumerate(starts):
-        copies[2 + i].wait()
-        for tile in range(start, start + GROUP):
-            at = slice(tile * width, (tile + 1) * width)
-            back = lax.dot_general(
-                weights_ref[tile], cot_ref[:, at], (((1,), (1,)), ((), ())), preferred_element_type=F32
-            ).T
-            back_ref[:, at] = jnp.where(first + tile < live, back, 0.0).astype(BF16)
+    for copy in copies[1:]:
+        copy.wait()
+    for tile in range(tiles):
+        at = slice(tile * width, (tile + 1) * width)
+        back = lax.dot_general(
+            weights_ref[tile], cot_ref[:, at], (((1,), (1,)), ((), ())), preferred_element_type=F32
+        ).T
+        back_ref[:, at] = jnp.where(first + tile < live, back, 0.0).astype(BF16)
 
 
 def back_blocks(live, cot, weights):
@@ -100,22 +96,29 @@
         pltpu.SMEM(live.shape, live.dtype),
         pltpu.VMEM(cot.shape, cot.dtype),
         pltpu.VMEM(weights.shape, weights.dtype),
-        pltpu.SemaphoreType.DMA((2 + weights.shape[0] // GROUP,)),
+        pltpu.SemaphoreType.DMA((3,)),
     ]
     return compiled(back_kernel, out, [hbm] * 3, "back_blocks", scratch, mib=53.55)(live, cot, weights)
 
 
-def sides_kernel(rows_ref, back_ref, out_ref):
-    out_ref[...] = scattered(rows_ref, back_ref, SIDES).astype(BF16)
+def sides_kernel(rows_ref, back_ref, give_ref, own_ref):
+    core = lax.axis_index("mem") % 2
+    both = scattered(rows_ref, back_ref, SIDES)
+    below, above = both[: both.shape[0] // 2], both[both.shape[0] // 2 :]
+    give_ref[...] = jnp.where(core == 0, below, above).astype(BF16)
+    own_ref[...] = jnp.where(core == 0, above, below)
 
 
 def sides_sums(rows, back):
     vmem = pl.BlockSpec(memory_space=pltpu.VMEM)
-    out = jax.ShapeDtypeStruct((len(SIDES) * back.shape[0], LANES), BF16)
+    shape = (CHUNKS * back.shape[0], LANES)
+    out = (jax.ShapeDtypeStruct(shape, BF16), jax.ShapeDtypeStruct(shape, F32))
     return compiled(sides_kernel, out, [vmem, vmem], "sides_sums")(rows, back)
 
 
-def inner_kernel(pert_ref, weights_ref, modes_ref, rows_ref, back_ref, out_ref, own_ref):
+def inner_kernel(
+    pert_ref, weights_ref, modes_ref, rows_ref, back_ref, give_ref, own_ref, sums_ref
+):
     members, levels, points = pert_ref.shape
     for chunk in range(CHUNKS):
         at = slice(chunk * LANES, (chunk + 1) * LANES)
@@ -128,53 +131,57 @@
                 preferred_element_type=F32,
             )
             total = total + pert_ref[k, :, at].astype(F32) * alpha
-        own_ref[chunk * levels : (chunk + 1) * levels, :] = total
-    own_ref[CHUNKS * levels :, :] = scattered(rows_ref, back_ref, CENTRE)
-    out_ref[...] = own_ref[...].astype(BF16)
+        sums_ref[chunk * levels : (chunk + 1) * levels, :] = total
+    sums_ref[CHUNKS * levels :, :] = scattered(rows_ref, back_ref, CENTRE)
+    core = lax.axis_index("mem") % 2
+    half = CHUNKS * levels // 2
+    for i in range(2):
+        at = slice(i * half, (i + 1) * half)
+        give = pl.multiple_of((2 * i + 1 - core) * half, half)
+        own = pl.multiple_of((2 * i + core) * half, half)
+        give_ref[at, :] = sums_ref[pl.ds(give, half), :].astype(BF16)
+        own_ref[at, :] = sums_ref[pl.ds(own, half), :]
 
 
 def inner_sums(pert, mode_weights, modes, rows, back):
     vmem = pl.BlockSpec(memory_space=pltpu.VMEM)
-    shape = (2 * CHUNKS * pert.shape[1], LANES)
+    shape = (CHUNKS * pert.shape[1], LANES)
     out = (jax.ShapeDtypeStruct(shape, BF16), jax.ShapeDtypeStruct(shape, F32))
-    return compiled(inner_kernel, out, [vmem] * 5, "inner_sums")(pert, mode_weights, modes, rows, back)
+    scratch = [pltpu.VMEM((2 * shape[0], LANES), F32)]
+    args = (pert, mode_weights, modes, rows, back)
+    return compiled(inner_kernel, out, [vmem] * 5, "inner_sums", scratch)(*args)
 
 
 def add(*refs):
-    return functools.reduce(jnp.add, [ref.astype(F32) for ref in refs])
-
-
-def outward_kernel(both_ref, out_ref):
-    size = out_ref.shape[0]
+    return functools.reduce(jnp.add, [ref[...].astype(F32) for ref in refs])
+
+
+def outward_kernel(given_ref, own_ref, out_ref):
     core = lax.axis_index("mem") % 2
-    at = pl.ds(pl.multiple_of((1 - core) * size, size), size)
-    out_ref[...] = add(both_ref[0, at, :], both_ref[1, at, :]).astype(BF16)
-
-
-def outward(both):
-    vmem = pl.BlockSpec(memory_space=pltpu.VMEM)
-    out = jax.ShapeDtypeStruct((both.shape[1] // 2, LANES), BF16)
-    return compiled(outward_kernel, out, [vmem], "outward", flops=10**6)(both)
-
-
-def chip_kernel(inner_ref, own_ref, came_ref, out_ref, exact_ref):
-    size = came_ref.shape[1]
-    half = size // 2
+    out_ref[...] = add(own_ref, given_ref.at[1 - core]).astype(BF16)
+
+
+def outward(given, own):
+    vmem = pl.BlockSpec(memory_space=pltpu.VMEM)
+    out = jax.ShapeDtypeStruct(own.shape, BF16)
+    return compiled(outward_kernel, out, [vmem, vmem], "outward", flops=10**6)(given, own)
+
+
+def chip_kernel(given_ref, own_ref, came_ref, out_ref, exact_ref):
+    half = came_ref.shape[1] // 2
     core = lax.axis_index("mem") % 2
     here = pl.ds(pl.multiple_of(core * half, half), half)
-    centre = pl.ds(pl.multiple_of(size + core * half, half), half)
-    exact_ref[:half, :] = add(own_ref[here, :], inner_ref[1 - core, here, :])
-    exact_ref[half:, :] = add(
-        own_ref[centre, :], inner_ref[1 - core, centre, :], came_ref[0, here, :], came_ref[1, here, :]
-    )
+    total = add(own_ref, given_ref.at[1 - core])
+    exact_ref[:half, :] = total[:half]
+    exact_ref[half:, :] = total[half:] + add(came_ref.at[0, here], came_ref.at[1, here])
     out_ref[...] = exact_ref[...].astype(BF16)
 
 
-def chip_sums(inner, own, came):
+def chip_sums(given, own, came):
     vmem = pl.BlockSpec(memory_space=pltpu.VMEM)
     shape = came.shape[1:]
     out = (jax.ShapeDtypeStruct(shape, BF16), jax.ShapeDtypeStruct(shape, F32))
-    return compiled(chip_kernel, out, [vmem] * 3, "chip_sums", flops=10**6)(inner, own, came)
+    return compiled(chip_kernel, out, [vmem] * 3, "chip_sums", flops=10**6)(given, own, came)
 
 
 def join_kernel(step, parts_ref, own_ref, out_ref, *exact_ref):
@@ -229,7 +236,9 @@
     return compiled(centre_kernel, out, [vmem, vmem], "centre_blocks")(rows, middle)
 
 
-def fine_kernel(kept_ref, rows_ref, weights_ref, centre_ref, sides_ref, out_ref, block_ref):
+def fine_kernel(
+    kept_ref, rows_ref, weights_ref, centre_ref, sides_ref, out_hbm, block_ref, out_ref, sems
+):
     tiles, width, _ = weights_ref.shape
     kept = kept_ref[:1, :]
     sides = jnp.concatenate([sides_ref[0], sides_ref[1]], axis=0)
@@ -237,17 +246,31 @@
         at = slice(tile * width, (tile + STEP) * width)
         rows = some_rows(rows_ref, tile, STEP)
         block_ref[:, at] = pick(sides, rows, centre_ref[:, at].astype(F32), SIDES)
-    for tile in range(tiles):
-        at = slice(tile * width, (tile + 1) * width)
-        fine = jnp.dot(block_ref[:, at], weights_ref[tile], preferred_element_type=F32)
-        out_ref[:, at] = jnp.where(tile < kept, fine, 0.0).astype(BF16)
+    copies = []
+    for start in range(0, tiles, GROUP):
+        for tile in range(start, start + GROUP):
+            at = slice(tile * width, (tile + 1) * width)
+            fine = jnp.dot(block_ref[:, at], weights_ref[tile], preferred_element_type=F32)
+            out_ref[:, at] = jnp.where(tile < kept, fine, 0.0).astype(BF16)
+        part = pl.ds(start * width, GROUP * width)
+        sem = sems.at[start // GROUP]
+        copies.append(pltpu.make_async_copy(out_ref.at[:, part], out_hbm.at[:, part], sem))
+        copies[-1].start()
+    for copy in copies:
+        copy.wait()
 
 
 def fine_sum(kept, rows, weights, blocks, sides):
     vmem = pl.BlockSpec(memory_space=pltpu.VMEM)
     out = jax.ShapeDtypeStruct(blocks.shape, BF16)
-    scratch = [pltpu.VMEM(blocks.shape, BF16)]
-    return compiled(fine_kernel, out, [vmem] * 5, "fine_sum", scratch)(kept, rows, weights, blocks, sides)
+    scratch = [
+        pltpu.VMEM(blocks.shape, BF16),
+        pltpu.VMEM(blocks.shape, BF16),
+        pltpu.SemaphoreType.DMA((weights.shape[0] // GROUP,)),
+    ]
+    hbm = pl.BlockSpec(memory_space=pltpu.HBM)
+    args = (kept, rows, weights, blocks, sides)
+    return compiled(fine_kernel, out, [vmem] * 5, "fine_sum", scratch, out_spec=hbm)(*args)
 
 
 def gradient_kernel(pert_ref, modes_ref, both_ref, out_ref):
@@ -314,9 +337,10 @@
 
     modes = vertical_modes.T
     back, kept = back_blocks(live_tiles, fine_cotangent, interp_weights)
-    came = to_bands(outward(to_pair(sides_sums(source_rows, back))))
-    inner, own = inner_sums(perturbations, mode_weights, modes, source_rows, back)
-    sums, own = chip_sums(to_pair(inner), own, to_pair(came))
+    give, own = sides_sums(source_rows, back)
+    came = to_bands(outward(to_pair(give), own))
+    give, own = inner_sums(perturbations, mode_weights, modes, source_rows, back)
+    sums, own = chip_sums(to_pair(give), own, to_pair(came))
     for step in range(2):
         parts = lax.all_gather(sums, "mem", axis_index_groups=chip_pairs(mems, step))
         sums, *own = join(step, parts, own)

time: 65.2 us -> 64.5 us (0.989)
  transfers between devices with their start and end apart: 2 -> 2, of which waited for: 0 -> 0; matrix products, arithmetic and copies ran while one was open for 0% -> 0% of each run, Pallas kernels for 5% -> 6%
where the time goes in v4:
time: 64.5 us; the launch traced here: 64.3 us
  blocking collectives  34.7 us (54%)
  starting transfers between devices  19 us (29%)
  Pallas kernels  9.12 us (14%)
  between operations  1.42 us (2%)
    all_gather x2, blocking collectives, shards(): lax.all_gather(sums, 'mem', axis_index_groups=chip_pairs(mems, step))  20.8 us
    ppermute x1, starting transfers between devices, shards(): came = to_bands(outward(to_pair(give), own))  13.8 us
    all_gather x1, blocking collectives, shards(): to_pair(came)  5.58 us
    ppermute x1, starting transfers between devices, shards(): came = to_bands(middle)  5.18 us
    all_gather x2, blocking collectives, shards(): sums, own = chip_sums(to_pair(give), own, to_pair(came))  3.98 us
    all_gather x1, blocking collectives, shards(): came = to_bands(outward(to_pair(give), own))  2.31 us
    pallas_call x1, Pallas kernels, fine_sum(): compiled(fine_kernel, out, [vmem] * 5, 'fine_sum', scratch, out_spec=hbm)  2.21 us
    all_gather x1, blocking collectives, shards(): both = to_pair(sums)  1.99 us
  transfers between devices with their start and end apart: 2, of which 0 were waited for; matrix products, arithmetic and copies ran while one was open for 0% of the time, Pallas kernels for 6%

profile of v4, /device:TPU:7, one launch (start us, length us, event | category | flops | bytes accessed | tf_op | source)
XLA Modules:
  0.0 64.3 jit_solution(14292253670986545979)
XLA Ops:
  1.3 0.0 copy-start.3
  1.3 1.8 %back_blocks.1 = (bf16[32,4096]{1,0:T(8,128)(2,1)S(1)}, s32[8,128]{1,0:T(8,128)S(1)}) custom-call(s32[1,1]{1,0:T(1,128)} %bitcast.9.live_hbm, bf16[32,4096]{1,0:T(8,128)(2,1)} %cot_hbm.1, bf16[32,128,128]{2,1,0:T(8,128)(2,1)} %weights_ref.3), custom_call_target="tpu_custom_call" | custom-call | flops 2000000000 | bytes 2000000 | tf_op jit(solution)/shard_map/back_blocks/pallas_call | solution.py:101
  3.1 0.0 copy-done.3
  3.1 0.0 copy-start
  3.1 0.0 copy-start.2
  3.1 0.0 copy-start.4
  3.2 1.3 %sides_sums.1 = (bf16[256,256]{1,0:T(8,128)(2,1)S(1)}, f32[256,256]{1,0:T(8,128)S(1)}) custom-call(s32[32,128]{1,0:T(8,128)S(1)} %copy-done.3, bf16[32,4096]{1,0:T(8,128)(2,1)S(1)} %get-tuple-element.13.back_ref), custom_call_target="tpu_custom_call" | custom-call | flops 2000000000 | bytes 2000000 | tf_op jit(solution)/shard_map/sides_sums/pallas_call | solution.py:116
  4.5 2.3 %all-gather.1 = bf16[512,256]{1,0:T(8,128)(2,1)S(1)} all-gather(bf16[256,256]{1,0:T(8,128)(2,1)S(1)} %get-tuple-element.16), channel_id=3, replica_groups={{0,1},{2,3},{4,5},{6,7},{8,9},{10,11},{12,13},{14,15},{16,17},{18,19},{..., dimensions={0}, use_global_device_ids=true | all-gather | bytes 393216 | tf_op jit(solution)/shard_map/all_gather | solution.py:341
  6.8 13.8 %collective-permute-start = (bf16[256,256]{1,0:T(8,128)(2,1)S(1)}, bf16[256,256]{1,0:T(8,128)(2,1)S(1)}, u32[]{:S(2)}, u32[]{:S(2)}) collective-permute-start(bf16[256,256]{1,0:T(8,128)(2,1)S(1)} %outward.1), channel_id=1, source_target_pairs={{0,8},{2,10},{4,12},{6,14},{8,16},{9,1},{10,18},{11,3},{12,20},{13... | collective-permute-start | bytes 393224 | tf_op jit(solution)/shard_map/ppermute | solution.py:341
  20.7 0.0 copy-done
  20.7 0.0 copy-done.2
  20.7 0.0 copy-done.4
  20.7 1.4 %inner_sums.1 = (bf16[256,256]{1,0:T(8,128)(2,1)S(1)}, f32[256,256]{1,0:T(8,128)S(1)}) custom-call(bf16[10,32,2048]{2,1,0:T(8,128)(2,1)S(1)} %copy-done, bf16[10,16,2048]{2,1,0:T(8,128)(2,1)S(1)} %copy-done.2, bf16[16,32]{1,0:T(8,128)(2,1)S(1)} %bitcast.18, s32[32,128]{1,0:T(8,128)S(1)} %copy-done.3, bf16[32,4096]{1,0:T(8,128)(2,1)S(1)} %get-tuple-element.13.back_ref), custom_call_target="tpu_custom_call" | custom-call | flops 2000000000 | bytes 2000000 | tf_op jit(solution)/shard_map/inner_sums/pallas_call | solution.py:152
  22.1 2.0 %all-gather = bf16[512,256]{1,0:T(8,128)(2,1)S(1)} all-gather(bf16[256,256]{1,0:T(8,128)(2,1)S(1)} %get-tuple-element.14), channel_id=2, replica_groups={{0,1},{2,3},{4,5},{6,7},{8,9},{10,11},{12,13},{14,15},{16,17},{18,19},{..., dimensions={0}, use_global_device_ids=true | all-gather | bytes 393216 | tf_op jit(solution)/shard_map/all_gather | solution.py:343
  24.1 0.0 collective-permute-done
  24.1 2.0 %all-gather.2 = bf16[512,256]{1,0:T(8,128)(2,1)S(1)} all-gather(bf16[256,256]{1,0:T(8,128)(2,1)S(1)} %collective-permute-done), channel_id=4, replica_groups={{0,1},{2,3},{4,5},{6,7},{8,9},{10,11},{12,13},{14,15},{16,17},{18,19},{..., dimensions={0}, use_global_device_ids=true | all-gather | bytes 393216 | tf_op jit(solution)/shard_map/all_gather | solution.py:343
  26.1 0.1 chip_sums.1
  26.2 12.4 %all-gather.3 = bf16[512,256]{1,0:T(8,128)(2,1)S(1)} all-gather(bf16[256,256]{1,0:T(8,128)(2,1)S(1)} %get-tuple-element.18), channel_id=5, replica_groups={{0,2},{4,6},{3,5},{7,1},{8,10},{12,14},{11,13},{15,9},{16,18},{20,22},{..., dimensions={0}, use_global_device_ids=true | all-gather | bytes 393216 | tf_op jit(solution)/shard_map/all_gather | solution.py:345
  38.6 8.4 %all-gather.4 = bf16[512,256]{1,0:T(8,128)(2,1)S(1)} all-gather(bf16[256,256]{1,0:T(8,128)(2,1)S(1)} %get-tuple-element.20), channel_id=6, replica_groups={{2,4},{6,0},{1,3},{5,7},{10,12},{14,8},{9,11},{13,15},{18,20},{22,16},{..., dimensions={0}, use_global_device_ids=true | all-gather | bytes 393216 | tf_op jit(solution)/shard_map/all_gather | solution.py:345
  47.1 2.0 %all-gather.5 = bf16[512,256]{1,0:T(8,128)(2,1)S(1)} all-gather(bf16[256,256]{1,0:T(8,128)(2,1)S(1)} %join.3), channel_id=7, replica_groups={{0,1},{2,3},{4,5},{6,7},{8,9},{10,11},{12,13},{14,15},{16,17},{18,19},{..., dimensions={0}, use_global_device_ids=true | all-gather | bytes 393216 | tf_op jit(solution)/shard_map/all_gather | solution.py:348
  49.1 5.2 %collective-permute-start.1 = (bf16[256,256]{1,0:T(8,128)(2,1)S(1)}, bf16[256,256]{1,0:T(8,128)(2,1)S(1)}, u32[]{:S(2)}, u32[]{:S(2)}) collective-permute-start(bf16[256,256]{1,0:T(8,128)(2,1)S(1)} %middle.1.middle_ref), channel_id=1, source_target_pairs={{0,8},{2,10},{4,12},{6,14},{8,16},{9,1},{10,18},{11,3},{12,20},{13... | collective-permute-start | bytes 393224 | tf_op jit(solution)/shard_map/ppermute | solution.py:350
  54.3 0.7 %centre_blocks.1.centre_ref = bf16[32,4096]{1,0:T(8,128)(2,1)S(1)} custom-call(s32[32,128]{1,0:T(8,128)S(1)} %copy-done.3, bf16[256,256]{1,0:T(8,128)(2,1)S(1)} %middle.1.middle_ref), custom_call_target="tpu_custom_call" | custom-call | flops 2000000000 | bytes 2000000 | tf_op jit(solution)/shard_map/centre_blocks/pallas_call | solution.py:236
  55.0 0.0 copy-start.1
  55.0 1.4 %gradient.1 = bf16[10,16,2048]{2,1,0:T(8,128)(2,1)} custom-call(bf16[10,32,2048]{2,1,0:T(8,128)(2,1)S(1)} %copy-done, bf16[16,32]{1,0:T(8,128)(2,1)S(1)} %bitcast.19, bf16[2,256,256]{2,1,0:T(8,128)(2,1)S(1)} %bitcast.13), custom_call_target="tpu_custom_call" | custom-call | flops 2000000000 | bytes 2000000 | tf_op jit(solution)/shard_map/gradient/pallas_call | solution.py:297
  56.5 0.0 collective-permute-done.1
  56.5 5.6 %all-gather.6 = bf16[512,256]{1,0:T(8,128)(2,1)S(1)} all-gather(bf16[256,256]{1,0:T(8,128)(2,1)S(1)} %collective-permute-done.1), channel_id=8, replica_groups={{0,1},{2,3},{4,5},{6,7},{8,9},{10,11},{12,13},{14,15},{16,17},{18,19},{..., dimensions={0}, use_global_device_ids=true | all-gather | bytes 393216 | tf_op jit(solution)/shard_map/all_gather | solution.py:353
  62.1 0.0 copy-done.1
  62.1 2.2 %fine_sum.1 = bf16[32,4096]{1,0:T(8,128)(2,1)} custom-call(s32[8,128]{1,0:T(8,128)S(1)} %get-tuple-element.12.kept_ref, s32[32,128]{1,0:T(8,128)S(1)} %copy-done.3, bf16[32,128,128]{2,1,0:T(8,128)(2,1)S(1)} %copy-done.1, bf16[32,4096]{1,0:T(8,128)(2,1)S(1)} %centre_blocks.1.centre_ref, bf16[2,256,256]{2,1,0:T(8,128)(2,1)S(1)} %bitcast.17), custom_call_target="tpu_custom_call" | custom-call | flops 2000000000 | bytes 2000000 | tf_op jit(solution)/shard_map/fine_sum/pallas_call | solution.py:273
  (4 shorter events, 0.1 us)
Async XLA Ops:
  1.3 1.8 %copy-start.3 = (s32[32,128]{1,0:T(8,128)S(1)}, s32[32,128]{1,0:T(8,128)}, u32[]{:S(2)}) copy-start(s32[32,128]{1,0:T(8,128)} %rows_ref.7) | copy-start | bytes 49156
  3.1 17.5 %copy-start = (bf16[10,32,2048]{2,1,0:T(8,128)(2,1)S(1)}, bf16[10,32,2048]{2,1,0:T(8,128)(2,1)}, u32[]{:S(2)}) copy-start(bf16[10,32,2048]{2,1,0:T(8,128)(2,1)} %pert_ref.3) | copy-start | bytes 3932164
  3.1 17.5 %copy-start.2 = (bf16[10,16,2048]{2,1,0:T(8,128)(2,1)S(1)}, bf16[10,16,2048]{2,1,0:T(8,128)(2,1)}, u32[]{:S(2)}) copy-start(bf16[10,16,2048]{2,1,0:T(8,128)(2,1)} %weights_ref.2) | copy-start | bytes 1966084
  3.1 17.5 %copy-start.4 = (bf16[32,16]{0,1:T(8,128)(2,1)S(1)}, bf16[32,16]{0,1:T(8,128)(2,1)}, u32[]{:S(2)}) copy-start(bf16[32,16]{0,1:T(8,128)(2,1)} %param.9) | copy-start | bytes 3076
  6.8 17.3 %collective-permute-start = (bf16[256,256]{1,0:T(8,128)(2,1)S(1)}, bf16[256,256]{1,0:T(8,128)(2,1)S(1)}, u32[]{:S(2)}, u32[]{:S(2)}) collective-permute-start(bf16[256,256]{1,0:T(8,128)(2,1)S(1)} %outward.1), channel_id=1, source_target_pairs={{0,8},{2,10},{4,12},{6,14},{8,16},{9,1},{10,18},{11,3},{12,20},{13... | collective-permute-start | bytes 393224 | tf_op jit(solution)/shard_map/ppermute | solution.py:341
  49.1 7.4 %collective-permute-start.1 = (bf16[256,256]{1,0:T(8,128)(2,1)S(1)}, bf16[256,256]{1,0:T(8,128)(2,1)S(1)}, u32[]{:S(2)}, u32[]{:S(2)}) collective-permute-start(bf16[256,256]{1,0:T(8,128)(2,1)S(1)} %middle.1.middle_ref), channel_id=1, source_target_pairs={{0,8},{2,10},{4,12},{6,14},{8,16},{9,1},{10,18},{11,3},{12,20},{13... | collective-permute-start | bytes 393224 | tf_op jit(solution)/shard_map/ppermute | solution.py:350
  55.0 7.0 %copy-start.1 = (bf16[32,128,128]{2,1,0:T(8,128)(2,1)S(1)}, bf16[32,128,128]{2,1,0:T(8,128)(2,1)}, u32[]{:S(2)}) copy-start(bf16[32,128,128]{2,1,0:T(8,128)(2,1)} %weights_ref.3) | copy-start | bytes 3145732

commit v5 on v4

--- a/solution.py
+++ b/solution.py
@@ -212,32 +212,37 @@
     return compiled(middle_kernel, out, [vmem], "middle", flops=10**6)(both)
 
 
-def pick(table, rows, block, chunks):
+def pick(table, rows, hot, block, chunks):
     levels = block.shape[0]
-    picked = jnp.dot(table, one_hot(rows), preferred_element_type=F32)
+    picked = jnp.dot(table, hot, preferred_element_type=F32)
     chunk = rows // LANES
     for i, k in enumerate(chunks):
         block = jnp.where(chunk == k, picked[i * levels : (i + 1) * levels], block)
     return block.astype(BF16)
 
 
-def centre_kernel(rows_ref, middle_ref, out_ref):
+def centre_kernel(rows_ref, middle_ref, out_ref, hot_ref):
     tiles, width = rows_ref.shape
     for tile in range(0, tiles, STEP):
         at = slice(tile * width, (tile + STEP) * width)
         none = jnp.zeros((out_ref.shape[0], STEP * width), F32)
         rows = some_rows(rows_ref, tile, STEP)
-        out_ref[:, at] = pick(middle_ref[...], rows, none, CENTRE)
+        hot = one_hot(rows)
+        hot_ref[:, at] = hot
+        out_ref[:, at] = pick(middle_ref[...], rows, hot, none, CENTRE)
 
 
 def centre_blocks(rows, middle):
     vmem = pl.BlockSpec(memory_space=pltpu.VMEM)
-    out = jax.ShapeDtypeStruct((middle.shape[0] // CHUNKS, rows.size), BF16)
+    out = (
+        jax.ShapeDtypeStruct((middle.shape[0] // CHUNKS, rows.size), BF16),
+        jax.ShapeDtypeStruct((LANES, rows.size), BF16),
+    )
     return compiled(centre_kernel, out, [vmem, vmem], "centre_blocks")(rows, middle)
 
 
 def fine_kernel(
-    kept_ref, rows_ref, weights_ref, centre_ref, sides_ref, out_hbm, block_ref, out_ref, sems
+    kept_ref, rows_ref, weights_ref, centre_ref, hot_ref, sides_ref, out_hbm, block_ref, out_ref, sems
 ):
     tiles, width, _ = weights_ref.shape
     kept = kept_ref[:1, :]
@@ -245,7 +250,7 @@
     for tile in range(0, tiles, STEP):
         at = slice(tile * width, (tile + STEP) * width)
         rows = some_rows(rows_ref, tile, STEP)
-        block_ref[:, at] = pick(sides, rows, centre_ref[:, at].astype(F32), SIDES)
+        block_ref[:, at] = pick(sides, rows, hot_ref[:, at], centre_ref[:, at].astype(F32), SIDES)
     copies = []
     for start in range(0, tiles, GROUP):
         for tile in range(start, start + GROUP):
@@ -260,7 +265,7 @@
         copy.wait()
 
 
-def fine_sum(kept, rows, weights, blocks, sides):
+def fine_sum(kept, rows, weights, blocks, hot, sides):
     vmem = pl.BlockSpec(memory_space=pltpu.VMEM)
     out = jax.ShapeDtypeStruct(blocks.shape, BF16)
     scratch = [
@@ -269,8 +274,8 @@
         pltpu.SemaphoreType.DMA((weights.shape[0] // GROUP,)),
     ]
     hbm = pl.BlockSpec(memory_space=pltpu.HBM)
-    args = (kept, rows, weights, blocks, sides)
-    return compiled(fine_kernel, out, [vmem] * 5, "fine_sum", scratch, out_spec=hbm)(*args)
+    args = (kept, rows, weights, blocks, hot, sides)
+    return compiled(fine_kernel, out, [vmem] * 6, "fine_sum", scratch, out_spec=hbm)(*args)
 
 
 def gradient_kernel(pert_ref, modes_ref, both_ref, out_ref):
@@ -349,8 +354,8 @@
     middle = middle_of(both)
     came = to_bands(middle)
     mode_gradient = gradient(perturbations, modes, both)
-    blocks = centre_blocks(source_rows, middle)
-    fine_increment = fine_sum(kept, source_rows, interp_weights, blocks, to_pair(came))
+    blocks, hot = centre_blocks(source_rows, middle)
+    fine_increment = fine_sum(kept, source_rows, interp_weights, blocks, hot, to_pair(came))
     return (fine_increment, mode_gradient)
 
 

time: 64.5 us -> 65.4 us (1.014)
  transfers between devices with their start and end apart: 2 -> 2, of which waited for: 0 -> 1; matrix products, arithmetic and copies ran while one was open for 0% -> 0% of each run, Pallas kernels for 6% -> 4%
where the time goes in v5:
time: 65.4 us; the launch traced here: 65.2 us
  blocking collectives  35 us (54%)
  starting transfers between devices  19.2 us (29%)
  Pallas kernels  9.1 us (14%)
  between operations  1.42 us (2%)
    all_gather x2, blocking collectives, shards(): lax.all_gather(sums, 'mem', axis_index_groups=chip_pairs(mems, step))  20.8 us
    ppermute x1, starting transfers between devices, shards(): came = to_bands(outward(to_pair(give), own))  13.8 us
    all_gather x1, blocking collectives, shards(): to_pair(came)  5.86 us
    ppermute x1, starting transfers between devices, shards(): came = to_bands(middle)  5.31 us
    all_gather x2, blocking collectives, shards(): sums, own = chip_sums(to_pair(give), own, to_pair(came))  3.98 us
    all_gather x1, blocking collectives, shards(): came = to_bands(outward(to_pair(give), own))  2.31 us
    pallas_call x1, Pallas kernels, fine_sum(): compiled(fine_kernel, out, [vmem] * 6, 'fine_sum', scratch, out_spec=hbm)  2.19 us
    all_gather x1, blocking collectives, shards(): both = to_pair(sums)  1.99 us
  transfers between devices with their start and end apart: 2, of which 1 were waited for; matrix products, arithmetic and copies ran while one was open for 0% of the time, Pallas kernels for 4%

profile of v5, /device:TPU:7, one launch (start us, length us, event | category | flops | bytes accessed | tf_op | source)
XLA Modules:
  0.0 65.2 jit_solution(16269029644786878791)
XLA Ops:
  1.3 0.0 copy-start.3
  1.3 1.8 %back_blocks.1 = (bf16[32,4096]{1,0:T(8,128)(2,1)S(1)}, s32[8,128]{1,0:T(8,128)S(1)}) custom-call(s32[1,1]{1,0:T(1,128)} %bitcast.9.live_hbm, bf16[32,4096]{1,0:T(8,128)(2,1)} %cot_hbm.1, bf16[32,128,128]{2,1,0:T(8,128)(2,1)} %weights_ref.3), custom_call_target="tpu_custom_call" | custom-call | flops 2000000000 | bytes 2000000 | tf_op jit(solution)/shard_map/back_blocks/pallas_call | solution.py:101
  3.1 0.0 copy-done.3
  3.1 0.0 copy-start
  3.1 0.0 copy-start.2
  3.1 0.0 copy-start.4
  3.2 1.3 %sides_sums.1 = (bf16[256,256]{1,0:T(8,128)(2,1)S(1)}, f32[256,256]{1,0:T(8,128)S(1)}) custom-call(s32[32,128]{1,0:T(8,128)S(1)} %copy-done.3, bf16[32,4096]{1,0:T(8,128)(2,1)S(1)} %get-tuple-element.15.back_ref), custom_call_target="tpu_custom_call" | custom-call | flops 2000000000 | bytes 2000000 | tf_op jit(solution)/shard_map/sides_sums/pallas_call | solution.py:116
  4.5 2.3 %all-gather.1 = bf16[512,256]{1,0:T(8,128)(2,1)S(1)} all-gather(bf16[256,256]{1,0:T(8,128)(2,1)S(1)} %get-tuple-element.18), channel_id=3, replica_groups={{0,1},{2,3},{4,5},{6,7},{8,9},{10,11},{12,13},{14,15},{16,17},{18,19},{..., dimensions={0}, use_global_device_ids=true | all-gather | bytes 393216 | tf_op jit(solution)/shard_map/all_gather | solution.py:346
  6.8 13.8 %collective-permute-start = (bf16[256,256]{1,0:T(8,128)(2,1)S(1)}, bf16[256,256]{1,0:T(8,128)(2,1)S(1)}, u32[]{:S(2)}, u32[]{:S(2)}) collective-permute-start(bf16[256,256]{1,0:T(8,128)(2,1)S(1)} %outward.1), channel_id=1, source_target_pairs={{0,8},{2,10},{4,12},{6,14},{8,16},{9,1},{10,18},{11,3},{12,20},{13... | collective-permute-start | bytes 393224 | tf_op jit(solution)/shard_map/ppermute | solution.py:346
  20.7 0.0 copy-done
  20.7 0.0 copy-done.2
  20.7 0.0 copy-done.4
  20.7 1.4 %inner_sums.1 = (bf16[256,256]{1,0:T(8,128)(2,1)S(1)}, f32[256,256]{1,0:T(8,128)S(1)}) custom-call(bf16[10,32,2048]{2,1,0:T(8,128)(2,1)S(1)} %copy-done, bf16[10,16,2048]{2,1,0:T(8,128)(2,1)S(1)} %copy-done.2, bf16[16,32]{1,0:T(8,128)(2,1)S(1)} %bitcast.18, s32[32,128]{1,0:T(8,128)S(1)} %copy-done.3, bf16[32,4096]{1,0:T(8,128)(2,1)S(1)} %get-tuple-element.15.back_ref), custom_call_target="tpu_custom_call" | custom-call | flops 2000000000 | bytes 2000000 | tf_op jit(solution)/shard_map/inner_sums/pallas_call | solution.py:152
  22.1 2.0 %all-gather = bf16[512,256]{1,0:T(8,128)(2,1)S(1)} all-gather(bf16[256,256]{1,0:T(8,128)(2,1)S(1)} %get-tuple-element.16), channel_id=2, replica_groups={{0,1},{2,3},{4,5},{6,7},{8,9},{10,11},{12,13},{14,15},{16,17},{18,19},{..., dimensions={0}, use_global_device_ids=true | all-gather | bytes 393216 | tf_op jit(solution)/shard_map/all_gather | solution.py:348
  24.1 0.0 collective-permute-done
  24.1 2.0 %all-gather.2 = bf16[512,256]{1,0:T(8,128)(2,1)S(1)} all-gather(bf16[256,256]{1,0:T(8,128)(2,1)S(1)} %collective-permute-done), channel_id=4, replica_groups={{0,1},{2,3},{4,5},{6,7},{8,9},{10,11},{12,13},{14,15},{16,17},{18,19},{..., dimensions={0}, use_global_device_ids=true | all-gather | bytes 393216 | tf_op jit(solution)/shard_map/all_gather | solution.py:348
  26.1 0.1 chip_sums.1
  26.2 12.4 %all-gather.3 = bf16[512,256]{1,0:T(8,128)(2,1)S(1)} all-gather(bf16[256,256]{1,0:T(8,128)(2,1)S(1)} %get-tuple-element.20), channel_id=5, replica_groups={{0,2},{4,6},{3,5},{7,1},{8,10},{12,14},{11,13},{15,9},{16,18},{20,22},{..., dimensions={0}, use_global_device_ids=true | all-gather | bytes 393216 | tf_op jit(solution)/shard_map/all_gather | solution.py:350
  38.6 8.4 %all-gather.4 = bf16[512,256]{1,0:T(8,128)(2,1)S(1)} all-gather(bf16[256,256]{1,0:T(8,128)(2,1)S(1)} %get-tuple-element.22), channel_id=6, replica_groups={{2,4},{6,0},{1,3},{5,7},{10,12},{14,8},{9,11},{13,15},{18,20},{22,16},{..., dimensions={0}, use_global_device_ids=true | all-gather | bytes 393216 | tf_op jit(solution)/shard_map/all_gather | solution.py:350
  47.1 2.0 %all-gather.5 = bf16[512,256]{1,0:T(8,128)(2,1)S(1)} all-gather(bf16[256,256]{1,0:T(8,128)(2,1)S(1)} %join.3), channel_id=7, replica_groups={{0,1},{2,3},{4,5},{6,7},{8,9},{10,11},{12,13},{14,15},{16,17},{18,19},{..., dimensions={0}, use_global_device_ids=true | all-gather | bytes 393216 | tf_op jit(solution)/shard_map/all_gather | solution.py:353
  49.1 0.8 %centre_blocks.1 = (bf16[32,4096]{1,0:T(8,128)(2,1)S(1)}, bf16[256,4096]{1,0:T(8,128)(2,1)S(1)}) custom-call(s32[32,128]{1,0:T(8,128)S(1)} %copy-done.3, bf16[256,256]{1,0:T(8,128)(2,1)S(1)} %middle.1.middle_ref), custom_call_target="tpu_custom_call" | custom-call | flops 2000000000 | bytes 2000000 | tf_op jit(solution)/shard_map/centre_blocks/pallas_call | solution.py:241
  49.9 0.0 copy-start.1
  49.9 5.3 %collective-permute-start.1 = (bf16[256,256]{1,0:T(8,128)(2,1)S(1)}, bf16[256,256]{1,0:T(8,128)(2,1)S(1)}, u32[]{:S(2)}, u32[]{:S(2)}) collective-permute-start(bf16[256,256]{1,0:T(8,128)(2,1)S(1)} %middle.1.middle_ref), channel_id=1, source_target_pairs={{0,8},{2,10},{4,12},{6,14},{8,16},{9,1},{10,18},{11,3},{12,20},{13... | collective-permute-start | bytes 393224 | tf_op jit(solution)/shard_map/ppermute | solution.py:355
  55.2 1.4 %gradient.1 = bf16[10,16,2048]{2,1,0:T(8,128)(2,1)} custom-call(bf16[10,32,2048]{2,1,0:T(8,128)(2,1)S(1)} %copy-done, bf16[16,32]{1,0:T(8,128)(2,1)S(1)} %bitcast.19, bf16[2,256,256]{2,1,0:T(8,128)(2,1)S(1)} %bitcast.13), custom_call_target="tpu_custom_call" | custom-call | flops 2000000000 | bytes 2000000 | tf_op jit(solution)/shard_map/gradient/pallas_call | solution.py:302
  56.6 0.5 collective-permute-done.1
  57.1 5.9 %all-gather.6 = bf16[512,256]{1,0:T(8,128)(2,1)S(1)} all-gather(bf16[256,256]{1,0:T(8,128)(2,1)S(1)} %collective-permute-done.1), channel_id=8, replica_groups={{0,1},{2,3},{4,5},{6,7},{8,9},{10,11},{12,13},{14,15},{16,17},{18,19},{..., dimensions={0}, use_global_device_ids=true | all-gather | bytes 393216 | tf_op jit(solution)/shard_map/all_gather | solution.py:358
  63.0 0.0 copy-done.1
  63.0 2.2 %fine_sum.1 = bf16[32,4096]{1,0:T(8,128)(2,1)} custom-call(s32[8,128]{1,0:T(8,128)S(1)} %get-tuple-element.14.kept_ref, s32[32,128]{1,0:T(8,128)S(1)} %copy-done.3, bf16[32,128,128]{2,1,0:T(8,128)(2,1)S(1)} %copy-done.1, bf16[32,4096]{1,0:T(8,128)(2,1)S(1)} %get-tuple-element.24.centre_ref, bf16[256,4096]{1,0:T(8,128)(2,1)S(1)} %get-tuple-element.25.hot_ref, ...), custom_call_target="tpu_custom_call" | custom-call | flops 2000000000 | bytes 2000000 | tf_op jit(solution)/shard_map/fine_sum/pallas_call | solution.py:278
  (4 shorter events, 0.1 us)
Async XLA Ops:
  1.3 1.8 %copy-start.3 = (s32[32,128]{1,0:T(8,128)S(1)}, s32[32,128]{1,0:T(8,128)}, u32[]{:S(2)}) copy-start(s32[32,128]{1,0:T(8,128)} %rows_ref.7) | copy-start | bytes 49156
  3.1 17.5 %copy-start = (bf16[10,32,2048]{2,1,0:T(8,128)(2,1)S(1)}, bf16[10,32,2048]{2,1,0:T(8,128)(2,1)}, u32[]{:S(2)}) copy-start(bf16[10,32,2048]{2,1,0:T(8,128)(2,1)} %pert_ref.3) | copy-start | bytes 3932164
  3.1 17.5 %copy-start.2 = (bf16[10,16,2048]{2,1,0:T(8,128)(2,1)S(1)}, bf16[10,16,2048]{2,1,0:T(8,128)(2,1)}, u32[]{:S(2)}) copy-start(bf16[10,16,2048]{2,1,0:T(8,128)(2,1)} %weights_ref.2) | copy-start | bytes 1966084
  3.1 17.5 %copy-start.4 = (bf16[32,16]{0,1:T(8,128)(2,1)S(1)}, bf16[32,16]{0,1:T(8,128)(2,1)}, u32[]{:S(2)}) copy-start(bf16[32,16]{0,1:T(8,128)(2,1)} %param.9) | copy-start | bytes 3076
  6.8 17.3 %collective-permute-start = (bf16[256,256]{1,0:T(8,128)(2,1)S(1)}, bf16[256,256]{1,0:T(8,128)(2,1)S(1)}, u32[]{:S(2)}, u32[]{:S(2)}) collective-permute-start(bf16[256,256]{1,0:T(8,128)(2,1)S(1)} %outward.1), channel_id=1, source_target_pairs={{0,8},{2,10},{4,12},{6,14},{8,16},{9,1},{10,18},{11,3},{12,20},{13... | collective-permute-start | bytes 393224 | tf_op jit(solution)/shard_map/ppermute | solution.py:346
  49.9 13.1 %copy-start.1 = (bf16[32,128,128]{2,1,0:T(8,128)(2,1)S(1)}, bf16[32,128,128]{2,1,0:T(8,128)(2,1)}, u32[]{:S(2)}) copy-start(bf16[32,128,128]{2,1,0:T(8,128)(2,1)} %weights_ref.3) | copy-start | bytes 3145732
  49.9 7.2 %collective-permute-start.1 = (bf16[256,256]{1,0:T(8,128)(2,1)S(1)}, bf16[256,256]{1,0:T(8,128)(2,1)S(1)}, u32[]{:S(2)}, u32[]{:S(2)}) collective-permute-start(bf16[256,256]{1,0:T(8,128)(2,1)S(1)} %middle.1.middle_ref), channel_id=1, source_target_pairs={{0,8},{2,10},{4,12},{6,14},{8,16},{9,1},{10,18},{11,3},{12,20},{13... | collective-permute-start | bytes 393224 | tf_op jit(solution)/shard_map/ppermute | solution.py:355

commit v6 on v4

--- a/solution.py
+++ b/solution.py
@@ -81,8 +81,8 @@
         at = slice(tile * width, (tile + 1) * width)
         back = lax.dot_general(
             weights_ref[tile], cot_ref[:, at], (((1,), (1,)), ((), ())), preferred_element_type=F32
-        ).T
-        back_ref[:, at] = jnp.where(first + tile < live, back, 0.0).astype(BF16)
+        )
+        back_ref[:, at] = jnp.where(first + tile < live, back, 0.0).astype(BF16).T
 
 
 def back_blocks(live, cot, weights):

time: 64.5 us -> 64.5 us (level)
  no operation moved by 1% of the time
where the time goes in v6:
time: 64.5 us; the launch traced here: 64.3 us
  blocking collectives  34.7 us (54%)
  starting transfers between devices  19 us (29%)
  Pallas kernels  9.09 us (14%)
  between operations  1.42 us (2%)
    all_gather x2, blocking collectives, shards(): lax.all_gather(sums, 'mem', axis_index_groups=chip_pairs(mems, step))  20.8 us
    ppermute x1, starting transfers between devices, shards(): came = to_bands(outward(to_pair(give), own))  13.8 us
    all_gather x1, blocking collectives, shards(): to_pair(came)  5.58 us
    ppermute x1, starting transfers between devices, shards(): came = to_bands(middle)  5.18 us
    all_gather x2, blocking collectives, shards(): sums, own = chip_sums(to_pair(give), own, to_pair(came))  3.98 us
    all_gather x1, blocking collectives, shards(): came = to_bands(outward(to_pair(give), own))  2.31 us
    pallas_call x1, Pallas kernels, fine_sum(): compiled(fine_kernel, out, [vmem] * 5, 'fine_sum', scratch, out_spec=hbm)  2.2 us
    all_gather x1, blocking collectives, shards(): both = to_pair(sums)  1.99 us
  transfers between devices with their start and end apart: 2, of which 0 were waited for; matrix products, arithmetic and copies ran while one was open for 0% of the time, Pallas kernels for 6%

profile of v6, /device:TPU:7, one launch (start us, length us, event | category | flops | bytes accessed | tf_op | source)
XLA Modules:
  0.0 64.3 jit_solution(4775863413285995453)
XLA Ops:
  1.3 0.0 copy-start.3
  1.3 1.8 %back_blocks.1 = (bf16[32,4096]{1,0:T(8,128)(2,1)S(1)}, s32[8,128]{1,0:T(8,128)S(1)}) custom-call(s32[1,1]{1,0:T(1,128)} %bitcast.9.live_hbm, bf16[32,4096]{1,0:T(8,128)(2,1)} %cot_hbm.1, bf16[32,128,128]{2,1,0:T(8,128)(2,1)} %weights_ref.3), custom_call_target="tpu_custom_call" | custom-call | flops 2000000000 | bytes 2000000 | tf_op jit(solution)/shard_map/back_blocks/pallas_call | solution.py:101
  3.1 0.0 copy-done.3
  3.1 0.0 copy-start
  3.1 0.0 copy-start.2
  3.1 0.0 copy-start.4
  3.1 1.3 %sides_sums.1 = (bf16[256,256]{1,0:T(8,128)(2,1)S(1)}, f32[256,256]{1,0:T(8,128)S(1)}) custom-call(s32[32,128]{1,0:T(8,128)S(1)} %copy-done.3, bf16[32,4096]{1,0:T(8,128)(2,1)S(1)} %get-tuple-element.13.back_ref), custom_call_target="tpu_custom_call" | custom-call | flops 2000000000 | bytes 2000000 | tf_op jit(solution)/shard_map/sides_sums/pallas_call | solution.py:116
  4.5 2.3 %all-gather.1 = bf16[512,256]{1,0:T(8,128)(2,1)S(1)} all-gather(bf16[256,256]{1,0:T(8,128)(2,1)S(1)} %get-tuple-element.16), channel_id=3, replica_groups={{0,1},{2,3},{4,5},{6,7},{8,9},{10,11},{12,13},{14,15},{16,17},{18,19},{..., dimensions={0}, use_global_device_ids=true | all-gather | bytes 393216 | tf_op jit(solution)/shard_map/all_gather | solution.py:341
  6.8 13.8 %collective-permute-start = (bf16[256,256]{1,0:T(8,128)(2,1)S(1)}, bf16[256,256]{1,0:T(8,128)(2,1)S(1)}, u32[]{:S(2)}, u32[]{:S(2)}) collective-permute-start(bf16[256,256]{1,0:T(8,128)(2,1)S(1)} %outward.1), channel_id=1, source_target_pairs={{0,8},{2,10},{4,12},{6,14},{8,16},{9,1},{10,18},{11,3},{12,20},{13... | collective-permute-start | bytes 393224 | tf_op jit(solution)/shard_map/ppermute | solution.py:341
  20.6 0.0 copy-done
  20.7 0.0 copy-done.2
  20.7 0.0 copy-done.4
  20.7 1.4 %inner_sums.1 = (bf16[256,256]{1,0:T(8,128)(2,1)S(1)}, f32[256,256]{1,0:T(8,128)S(1)}) custom-call(bf16[10,32,2048]{2,1,0:T(8,128)(2,1)S(1)} %copy-done, bf16[10,16,2048]{2,1,0:T(8,128)(2,1)S(1)} %copy-done.2, bf16[16,32]{1,0:T(8,128)(2,1)S(1)} %bitcast.18, s32[32,128]{1,0:T(8,128)S(1)} %copy-done.3, bf16[32,4096]{1,0:T(8,128)(2,1)S(1)} %get-tuple-element.13.back_ref), custom_call_target="tpu_custom_call" | custom-call | flops 2000000000 | bytes 2000000 | tf_op jit(solution)/shard_map/inner_sums/pallas_call | solution.py:152
  22.1 2.0 %all-gather = bf16[512,256]{1,0:T(8,128)(2,1)S(1)} all-gather(bf16[256,256]{1,0:T(8,128)(2,1)S(1)} %get-tuple-element.14), channel_id=2, replica_groups={{0,1},{2,3},{4,5},{6,7},{8,9},{10,11},{12,13},{14,15},{16,17},{18,19},{..., dimensions={0}, use_global_device_ids=true | all-gather | bytes 393216 | tf_op jit(solution)/shard_map/all_gather | solution.py:343
  24.1 0.0 collective-permute-done
  24.1 2.0 %all-gather.2 = bf16[512,256]{1,0:T(8,128)(2,1)S(1)} all-gather(bf16[256,256]{1,0:T(8,128)(2,1)S(1)} %collective-permute-done), channel_id=4, replica_groups={{0,1},{2,3},{4,5},{6,7},{8,9},{10,11},{12,13},{14,15},{16,17},{18,19},{..., dimensions={0}, use_global_device_ids=true | all-gather | bytes 393216 | tf_op jit(solution)/shard_map/all_gather | solution.py:343
  26.1 0.1 chip_sums.1
  26.2 12.4 %all-gather.3 = bf16[512,256]{1,0:T(8,128)(2,1)S(1)} all-gather(bf16[256,256]{1,0:T(8,128)(2,1)S(1)} %get-tuple-element.18), channel_id=5, replica_groups={{0,2},{4,6},{3,5},{7,1},{8,10},{12,14},{11,13},{15,9},{16,18},{20,22},{..., dimensions={0}, use_global_device_ids=true | all-gather | bytes 393216 | tf_op jit(solution)/shard_map/all_gather | solution.py:345
  38.6 8.4 %all-gather.4 = bf16[512,256]{1,0:T(8,128)(2,1)S(1)} all-gather(bf16[256,256]{1,0:T(8,128)(2,1)S(1)} %get-tuple-element.20), channel_id=6, replica_groups={{2,4},{6,0},{1,3},{5,7},{10,12},{14,8},{9,11},{13,15},{18,20},{22,16},{..., dimensions={0}, use_global_device_ids=true | all-gather | bytes 393216 | tf_op jit(solution)/shard_map/all_gather | solution.py:345
  47.1 2.0 %all-gather.5 = bf16[512,256]{1,0:T(8,128)(2,1)S(1)} all-gather(bf16[256,256]{1,0:T(8,128)(2,1)S(1)} %join.3), channel_id=7, replica_groups={{0,1},{2,3},{4,5},{6,7},{8,9},{10,11},{12,13},{14,15},{16,17},{18,19},{..., dimensions={0}, use_global_device_ids=true | all-gather | bytes 393216 | tf_op jit(solution)/shard_map/all_gather | solution.py:348
  49.1 5.2 %collective-permute-start.1 = (bf16[256,256]{1,0:T(8,128)(2,1)S(1)}, bf16[256,256]{1,0:T(8,128)(2,1)S(1)}, u32[]{:S(2)}, u32[]{:S(2)}) collective-permute-start(bf16[256,256]{1,0:T(8,128)(2,1)S(1)} %middle.1.middle_ref), channel_id=1, source_target_pairs={{0,8},{2,10},{4,12},{6,14},{8,16},{9,1},{10,18},{11,3},{12,20},{13... | collective-permute-start | bytes 393224 | tf_op jit(solution)/shard_map/ppermute | solution.py:350
  54.3 0.7 %centre_blocks.1.centre_ref = bf16[32,4096]{1,0:T(8,128)(2,1)S(1)} custom-call(s32[32,128]{1,0:T(8,128)S(1)} %copy-done.3, bf16[256,256]{1,0:T(8,128)(2,1)S(1)} %middle.1.middle_ref), custom_call_target="tpu_custom_call" | custom-call | flops 2000000000 | bytes 2000000 | tf_op jit(solution)/shard_map/centre_blocks/pallas_call | solution.py:236
  55.0 0.0 copy-start.1
  55.0 1.4 %gradient.1 = bf16[10,16,2048]{2,1,0:T(8,128)(2,1)} custom-call(bf16[10,32,2048]{2,1,0:T(8,128)(2,1)S(1)} %copy-done, bf16[16,32]{1,0:T(8,128)(2,1)S(1)} %bitcast.19, bf16[2,256,256]{2,1,0:T(8,128)(2,1)S(1)} %bitcast.13), custom_call_target="tpu_custom_call" | custom-call | flops 2000000000 | bytes 2000000 | tf_op jit(solution)/shard_map/gradient/pallas_call | solution.py:297
  56.5 0.0 collective-permute-done.1
  56.5 5.6 %all-gather.6 = bf16[512,256]{1,0:T(8,128)(2,1)S(1)} all-gather(bf16[256,256]{1,0:T(8,128)(2,1)S(1)} %collective-permute-done.1), channel_id=8, replica_groups={{0,1},{2,3},{4,5},{6,7},{8,9},{10,11},{12,13},{14,15},{16,17},{18,19},{..., dimensions={0}, use_global_device_ids=true | all-gather | bytes 393216 | tf_op jit(solution)/shard_map/all_gather | solution.py:353
  62.1 0.0 copy-done.1
  62.1 2.2 %fine_sum.1 = bf16[32,4096]{1,0:T(8,128)(2,1)} custom-call(s32[8,128]{1,0:T(8,128)S(1)} %get-tuple-element.12.kept_ref, s32[32,128]{1,0:T(8,128)S(1)} %copy-done.3, bf16[32,128,128]{2,1,0:T(8,128)(2,1)S(1)} %copy-done.1, bf16[32,4096]{1,0:T(8,128)(2,1)S(1)} %centre_blocks.1.centre_ref, bf16[2,256,256]{2,1,0:T(8,128)(2,1)S(1)} %bitcast.17), custom_call_target="tpu_custom_call" | custom-call | flops 2000000000 | bytes 2000000 | tf_op jit(solution)/shard_map/fine_sum/pallas_call | solution.py:273
  (4 shorter events, 0.1 us)
Async XLA Ops:
  1.3 1.8 %copy-start.3 = (s32[32,128]{1,0:T(8,128)S(1)}, s32[32,128]{1,0:T(8,128)}, u32[]{:S(2)}) copy-start(s32[32,128]{1,0:T(8,128)} %rows_ref.7) | copy-start | bytes 49156
  3.1 17.5 %copy-start = (bf16[10,32,2048]{2,1,0:T(8,128)(2,1)S(1)}, bf16[10,32,2048]{2,1,0:T(8,128)(2,1)}, u32[]{:S(2)}) copy-start(bf16[10,32,2048]{2,1,0:T(8,128)(2,1)} %pert_ref.3) | copy-start | bytes 3932164
  3.1 17.5 %copy-start.2 = (bf16[10,16,2048]{2,1,0:T(8,128)(2,1)S(1)}, bf16[10,16,2048]{2,1,0:T(8,128)(2,1)}, u32[]{:S(2)}) copy-start(bf16[10,16,2048]{2,1,0:T(8,128)(2,1)} %weights_ref.2) | copy-start | bytes 1966084
  3.1 17.5 %copy-start.4 = (bf16[32,16]{0,1:T(8,128)(2,1)S(1)}, bf16[32,16]{0,1:T(8,128)(2,1)}, u32[]{:S(2)}) copy-start(bf16[32,16]{0,1:T(8,128)(2,1)} %param.9) | copy-start | bytes 3076
  6.8 17.3 %collective-permute-start = (bf16[256,256]{1,0:T(8,128)(2,1)S(1)}, bf16[256,256]{1,0:T(8,128)(2,1)S(1)}, u32[]{:S(2)}, u32[]{:S(2)}) collective-permute-start(bf16[256,256]{1,0:T(8,128)(2,1)S(1)} %outward.1), channel_id=1, source_target_pairs={{0,8},{2,10},{4,12},{6,14},{8,16},{9,1},{10,18},{11,3},{12,20},{13... | collective-permute-start | bytes 393224 | tf_op jit(solution)/shard_map/ppermute | solution.py:341
  49.1 7.4 %collective-permute-start.1 = (bf16[256,256]{1,0:T(8,128)(2,1)S(1)}, bf16[256,256]{1,0:T(8,128)(2,1)S(1)}, u32[]{:S(2)}, u32[]{:S(2)}) collective-permute-start(bf16[256,256]{1,0:T(8,128)(2,1)S(1)} %middle.1.middle_ref), channel_id=1, source_target_pairs={{0,8},{2,10},{4,12},{6,14},{8,16},{9,1},{10,18},{11,3},{12,20},{13... | collective-permute-start | bytes 393224 | tf_op jit(solution)/shard_map/ppermute | solution.py:350
  55.0 7.0 %copy-start.1 = (bf16[32,128,128]{2,1,0:T(8,128)(2,1)S(1)}, bf16[32,128,128]{2,1,0:T(8,128)(2,1)}, u32[]{:S(2)}) copy-start(bf16[32,128,128]{2,1,0:T(8,128)(2,1)} %weights_ref.3) | copy-start | bytes 3145732
